TPU v7x, 32 devices: a whole 2x2x4 slice. The times are simulated.
32 devices in a mesh: gx: 8 (over y, x, core), gy: 4 (over z).
Axes of the slice: x: 2, y: 2, z: 4, core: 2. Of those that a mesh axis runs over, the one named last changes fastest.
Arguments:
- body_force: float32 [3, 256, 128, 128], P(None, 'gx', 'gy'), may hold values from -8 to 8
- shift_coef: float32 [256, 128, 128], P('gx', 'gy'), may hold values from 0.25 to 2
- coupling: float32 [7776, 1024], P(None, ('gx', 'gy')), may hold values from -0.625 to 0.625
- node_cells: int32 [32, 1024], P(None, ('gx', 'gy')), may hold values from 0 to 131071
- target_gap: float32 [81, 1024], P(None, ('gx', 'gy')), may hold values from -4 to 4
- new_owner: int32 [1024, 1], P(('gx', 'gy')), may hold values from 0 to 7; in each aligned block of 32 rows (0 to 31, 32 to 63, ...) at most 4 rows name the same one
Outputs:
- multipliers: float32 [81, 1024], P(None, ('gx', 'gy'))
- velocity: float32 [3, 256, 128, 128], P(None, 'gx', 'gy')
Inputs may be any that keep to these rules, and one draw needn't show every extreme that they name: `new_owner`: among the 32 elements of one device, at most 4 name the same new owner, and exactly 4 do for some owner.
All inputs are finite; a program needn't handle non-finite values.
Results may differ from a plain program's by a relative error of at most 0.0003.
Values sent between devices are 32-bit elements; how exact they have to be, the bound alone decides.
A program may use at most 64 MiB of HBM per device.

v0:
```python
import jax
import jax.numpy as jnp
from jax import lax
from jax.sharding import PartitionSpec as P

COMP = 3
NODES = 32
MULT = 81
ITERS = 4


def padded_2(cells, sides, width):
    for axis, dim in sides:
        count = lax.axis_size(axis)
        ends = count - 1
        head = lax.slice_in_dim(cells, 0, width, axis=dim)
        tail = lax.slice_in_dim(cells, cells.shape[dim] - width, cells.shape[dim], axis=dim)
        cells = jnp.concatenate(
            [
                lax.ppermute(tail, axis, [(i, (i + 1) % count) for i in range(ends)]),
                cells,
                lax.ppermute(head, axis, [((i + 1) % count, i) for i in range(ends)]),
            ],
            axis=dim,
        )
    return cells


def operate(fluid_field, shift_coef):
    padded = padded_2(fluid_field, (("gx", 1), ("gy", 2)), 1)
    padded = jnp.pad(padded, ((0, 0), (0, 0), (0, 0), (1, 1)))
    beside = padded[:, 2:, 1:-1, 1:-1] + padded[:, :-2, 1:-1, 1:-1]
    beside = beside + padded[:, 1:-1, 2:, 1:-1] + padded[:, 1:-1, :-2, 1:-1]
    beside = beside + padded[:, 1:-1, 1:-1, 2:] + padded[:, 1:-1, 1:-1, :-2]
    return (6.0 + shift_coef) * fluid_field - beside


def smooth(residual_in, shift_coef):
    diagonal = 6.0 + shift_coef
    first_pass = residual_in / diagonal
    return first_pass + (residual_in - operate(first_pass, shift_coef)) / diagonal


def total_squares(residual):
    return lax.psum(jnp.sum(residual * residual), ("gx", "gy"))


def shards(body_force, shift_coef, coupling, node_cells, target_gap, new_owner):
    local_elems = coupling.shape[1]
    groups = lax.axis_size("gx")
    capacity = local_elems // 8
    slot_count = groups * capacity
    owners = new_owner[:, 0]
    onehot = (owners[:, None] == jnp.arange(groups, dtype=jnp.int32)[None, :]).astype(jnp.int32)
    rank_in = jnp.sum((jnp.cumsum(onehot, axis=0) - 1) * onehot, axis=1)
    slot_of = owners * capacity + rank_in
    cell_total = body_force.shape[1] * body_force.shape[2] * body_force.shape[3]
    block_rows = COMP * NODES

    def place(columns):
        return jnp.zeros((columns.shape[0], slot_count), columns.dtype).at[:, slot_of].set(columns)

    def spread(term_cols, dof_index):
        flat = (
            jnp.zeros((COMP * cell_total,), jnp.float32)
            .at[dof_index.reshape(-1)]
            .add(term_cols.reshape(-1))
        )
        return flat.reshape(body_force.shape)

    def collect(fluid_field, dof_index):
        return fluid_field.reshape(-1)[dof_index]

    moved, moved_cells, moved_goal = (
        lax.all_to_all(place(coupling), "gx", split_axis=1, concat_axis=1, tiled=True),
        lax.all_to_all(
            place(node_cells.astype(jnp.float32)), "gx", split_axis=1, concat_axis=1, tiled=True
        ),
        lax.all_to_all(place(target_gap), "gx", split_axis=1, concat_axis=1, tiled=True),
    )
    blocks = moved.reshape(block_rows, MULT, slot_count)
    cell_int = moved_cells.astype(jnp.int32)
    dof_index = (
        jnp.arange(COMP, dtype=jnp.int32)[:, None, None] * cell_total + cell_int[None]
    ).reshape(block_rows, -1)

    def apply_bt(multi):
        term_cols = jnp.einsum("ams,ms->as", blocks, multi, precision=lax.Precision.HIGHEST)
        return spread(term_cols, dof_index)

    def apply_b(fluid_field):
        return jnp.einsum(
            "ams,as->ms", blocks, collect(fluid_field, dof_index), precision=lax.Precision.HIGHEST
        )

    goal_vals = apply_b(smooth(body_force, shift_coef)) - moved_goal
    multipliers = jnp.zeros_like(goal_vals)
    residual = goal_vals
    direction = goal_vals
    norm_now = total_squares(residual)
    for iteration in range(ITERS):
        image = apply_b(smooth(apply_bt(direction), shift_coef))
        step_size = norm_now / lax.psum(jnp.sum(direction * image), ("gx", "gy"))
        multipliers = multipliers + step_size * direction
        residual = residual - step_size * image
        norm_next = total_squares(residual)
        direction = residual + norm_next / norm_now * direction
        norm_now = norm_next
    velocity = smooth(body_force - apply_bt(multipliers), shift_coef)
    multipliers = lax.all_to_all(multipliers, "gx", split_axis=1, concat_axis=1, tiled=True)[
        :, slot_of
    ]
    return (multipliers, velocity)


def solution(mesh):
    in_specs = (
        P(None, "gx", "gy", None),
        P("gx", "gy", None),
        P(None, ("gx", "gy")),
        P(None, ("gx", "gy")),
        P(None, ("gx", "gy")),
        P(("gx", "gy"), None),
    )
    out_specs = (P(None, ("gx", "gy")), P(None, "gx", "gy", None))
    return jax.shard_map(shards, mesh=mesh, in_specs=in_specs, out_specs=out_specs, check_vma=False)
```

profile of v0, /device:TPU:0, one launch (start us, length us, event | category | flops | bytes accessed | tf_op | source)
XLA Modules:
  0.0 680.3 jit_solution(11187794397832491853)
XLA Ops:
  9.6 5.8 all-to-all-start
  21.5 4.2 all-to-all-start.1
  29.0 4.5 collective-permute-start.3
  38.9 5.5 fusion.39
  44.4 17.4 %gather_fusion = f32[3072]{0:T(1024)S(1)} fusion(f32[393216]{0:T(1024)S(1)} %bitcast.117, s32[3072]{0:T(1024)S(1)} %broadcast_clamp_fusion), kind=kCustom, calls=%fused_computation | custom fusion | bytes 36864 | tf_op jit(solution)/shard_map/gather | solution.py:72
  61.9 4.7 all-to-all-start.2
  66.7 3.8 reshape.150
  74.7 17.0 %scatter_custom_fusion.3 = f32[393216]{0:T(1024)S(1)} fusion(s32[3072]{0:T(1024)S(1)} %bitcast.153, f32[3072]{0:T(1024)S(1)} %reshape.241, f32[]{:T(128)} %constant.9.clone.1), kind=kCustom, calls=%fused_computation.153 | custom fusion | flops 3072 | bytes 1572868 | tf_op jit(solution)/shard_map/scatter-add | solution.py:67
  99.4 5.0 collective-permute-start.7
  106.2 3.6 select_maximum_fusion.16
  112.5 17.4 %gather_fusion.1 = f32[3072]{0:T(1024)S(1)} fusion(f32[393216]{0:T(1024)S(1)} %bitcast.114, s32[3072]{0:T(1024)S(1)} %broadcast_clamp_fusion), kind=kCustom, calls=%fused_computation.1 | custom fusion | bytes 36864 | tf_op jit(solution)/shard_map/gather | solution.py:72
  133.6 45.4 %all-reduce.6 = (f32[]{:T(128)}, f32[]{:T(128)}) all-reduce(f32[]{:T(128)} %get-tuple-element.3, f32[]{:T(128)} %get-tuple-element.2), channel_id=1, replica_groups=mesh['gx'=8,'gy'=4] {'gx','gy'}, use_global_device_ids=true, to_apply=%region_6.7 | all-reduce | flops 2 | bytes 16 | tf_op jit(solution)/shard_map/psum | solution.py:45
  181.0 41.9 %psum.58 = f32[]{:T(128)} all-reduce(f32[]{:T(128)} %multiply_reduce_fusion.5), channel_id=1, replica_groups=mesh['gx'=8,'gy'=4] {'gx','gy'}, use_global_device_ids=true, to_apply=%region_11.12 | all-reduce | flops 1 | bytes 8 | tf_op jit(solution)/shard_map/psum | solution.py:45
  226.9 17.0 %scatter_custom_fusion.4 = f32[393216]{0:T(1024)S(1)} fusion(s32[3072]{0:T(1024)S(1)} %bitcast.154, f32[3072]{0:T(1024)S(1)} %reshape.249, f32[]{:T(128)} %constant.9.clone.1), kind=kCustom, calls=%fused_computation.151 | custom fusion | flops 3072 | bytes 1572868 | tf_op jit(solution)/shard_map/scatter-add | solution.py:67
  251.6 4.7 collective-permute-start.11
  258.1 3.6 select_maximum_fusion.12
  264.4 17.4 %gather_fusion.2 = f32[3072]{0:T(1024)S(1)} fusion(f32[393216]{0:T(1024)S(1)} %bitcast.115, s32[3072]{0:T(1024)S(1)} %broadcast_clamp_fusion), kind=kCustom, calls=%fused_computation.2 | custom fusion | bytes 36864 | tf_op jit(solution)/shard_map/gather | solution.py:72
  285.5 43.8 %psum.59 = f32[]{:T(128)} all-reduce(f32[]{:T(128)} %multiply_reduce_fusion.4), channel_id=1, replica_groups=mesh['gx'=8,'gy'=4] {'gx','gy'}, use_global_device_ids=true, to_apply=%region_14.15 | all-reduce | flops 1 | bytes 8 | tf_op jit(solution)/shard_map/psum | solution.py:103
  331.3 41.0 %psum.60 = f32[]{:T(128)} all-reduce(f32[]{:T(128)} %get-tuple-element.8), channel_id=1, replica_groups=mesh['gx'=8,'gy'=4] {'gx','gy'}, use_global_device_ids=true, to_apply=%region_16.17 | all-reduce | flops 1 | bytes 8 | tf_op jit(solution)/shard_map/psum | solution.py:45
  376.3 17.0 %scatter_custom_fusion.5 = f32[393216]{0:T(1024)S(1)} fusion(s32[3072]{0:T(1024)S(1)} %bitcast.155, f32[3072]{0:T(1024)S(1)} %reshape.257, f32[]{:T(128)} %constant.9.clone.1), kind=kCustom, calls=%fused_computation.149 | custom fusion | flops 3072 | bytes 1572868 | tf_op jit(solution)/shard_map/scatter-add | solution.py:67
  401.0 4.7 collective-permute-start.15
  413.8 17.4 %gather_fusion.3 = f32[3072]{0:T(1024)S(1)} fusion(f32[393216]{0:T(1024)S(1)} %bitcast.116, s32[3072]{0:T(1024)S(1)} %broadcast_clamp_fusion), kind=kCustom, calls=%fused_computation.3 | custom fusion | bytes 36864 | tf_op jit(solution)/shard_map/gather | solution.py:72
  434.9 44.0 %psum.61 = f32[]{:T(128)} all-reduce(f32[]{:T(128)} %multiply_reduce_fusion.2), channel_id=1, replica_groups=mesh['gx'=8,'gy'=4] {'gx','gy'}, use_global_device_ids=true, to_apply=%region_19.20 | all-reduce | flops 1 | bytes 8 | tf_op jit(solution)/shard_map/psum | solution.py:103
  480.8 41.4 %psum.62 = f32[]{:T(128)} all-reduce(f32[]{:T(128)} %multiply_reduce_fusion.1), channel_id=1, replica_groups=mesh['gx'=8,'gy'=4] {'gx','gy'}, use_global_device_ids=true, to_apply=%region_21.22 | all-reduce | flops 1 | bytes 8 | tf_op jit(solution)/shard_map/psum | solution.py:45
  526.2 17.0 %scatter_custom_fusion.6 = f32[393216]{0:T(1024)S(1)} fusion(s32[3072]{0:T(1024)S(1)} %bitcast.156, f32[3072]{0:T(1024)S(1)} %reshape.265, f32[]{:T(128)} %constant.9.clone.1), kind=kCustom, calls=%fused_computation.147 | custom fusion | flops 3072 | bytes 1572868 | tf_op jit(solution)/shard_map/scatter-add | solution.py:67
  550.9 4.7 collective-permute-start.19
  563.7 17.4 %gather_fusion.4 = f32[3072]{0:T(1024)S(1)} fusion(f32[393216]{0:T(1024)S(1)} %bitcast.113, s32[3072]{0:T(1024)S(1)} %broadcast_clamp_fusion), kind=kCustom, calls=%fused_computation.4 | custom fusion | bytes 36864 | tf_op jit(solution)/shard_map/gather | solution.py:72
  584.8 44.0 %psum.63 = f32[]{:T(128)} all-reduce(f32[]{:T(128)} %multiply_reduce_fusion), channel_id=1, replica_groups=mesh['gx'=8,'gy'=4] {'gx','gy'}, use_global_device_ids=true, to_apply=%region_24.25 | all-reduce | flops 1 | bytes 8 | tf_op jit(solution)/shard_map/psum | solution.py:103
  634.2 17.8 %scatter_custom_fusion.7 = f32[393216]{0:T(1024)} fusion(s32[3072]{0:T(1024)S(1)} %bitcast.157, f32[3072]{0:T(1024)S(1)} %reshape.273, f32[]{:T(128)} %constant.9.clone.1), kind=kCustom, calls=%fused_computation.145 | custom fusion | flops 3072 | bytes 1572868 | tf_op jit(solution)/shard_map/scatter-add | solution.py:67
  651.9 3.7 broadcast_divide_fusion
  660.0 5.2 all-to-all-start.3
  666.6 4.5 collective-permute-start.23
  (185 shorter events, 126.9 us)
Async XLA Ops:
  3.5 24.0 %collective-permute-start = (f32[3,1,32,128]{3,2,1,0:T(8,128)S(1)}, f32[3,1,32,128]{3,2,1,0:T(8,128)S(1)}, u32[]{:S(2)}, u32[]{:S(2)}) collective-permute-start(f32[3,1,32,128]{3,2,1,0:T(8,128)S(1)} %get-tuple-element.33), channel_id=1, source_target_pairs={{4,0},{8,4},{12,8},{16,12},{20,16},{24,20},{28,24},{5,1},{9,5},{13... | collective-permute-start | bytes 147464 | tf_op jit(solution)/shard_map/ppermute | solution.py:22
  4.8 22.7 %collective-permute-start.1 = (f32[3,1,32,128]{3,2,1,0:T(8,128)S(1)}, f32[3,1,32,128]{3,2,1,0:T(8,128)S(1)}, u32[]{:S(2)}, u32[]{:S(2)}) collective-permute-start(f32[3,1,32,128]{3,2,1,0:T(8,128)S(1)} %get-tuple-element.32), channel_id=1, source_target_pairs={{0,4},{4,8},{8,12},{12,16},{16,20},{20,24},{24,28},{1,5},{5,9},{9,... | collective-permute-start | bytes 147464 | tf_op jit(solution)/shard_map/ppermute | solution.py:20
  9.6 11.8 %all-to-all-start = ((f32[8,1,128]{2,1,0:T(1,128)}), f32[8,1,128]{2,1,0:T(1,128)S(1)}, u32[]{:S(2)}, u32[]{:S(2)}) async-start(f32[8,1,128]{2,1,0:T(1,128)} %reshape.323), calls=%async_computation | async-start | bytes 8192 | tf_op jit(solution)/shard_map/all_to_all | solution.py:76
  21.5 40.5 %all-to-all-start.1 = ((f32[7776,8,4]{0,2,1:T(4,128)}), f32[7776,8,4]{0,2,1:T(4,128)}, u32[]{:S(2)}, u32[]{:S(2)}) async-start(f32[7776,8,4]{0,2,1:T(4,128)} %all_to_all.30), calls=%async_computation.1 | async-start | bytes 1998848 | tf_op jit(solution)/shard_map/all_to_all | solution.py:75
  27.7 6.1 collective-permute-start.2
  29.0 6.3 collective-permute-start.3
  61.9 10.0 %all-to-all-start.2 = ((f32[81,8,4]{0,2,1:T(4,128)}), f32[81,8,4]{0,2,1:T(4,128)S(1)}, u32[]{:S(2)}, u32[]{:S(2)}) async-start(f32[81,8,4]{0,2,1:T(4,128)} %bitcast.13), calls=%async_computation.2 | async-start | bytes 32768 | tf_op jit(solution)/shard_map/all_to_all | solution.py:79
  92.8 4.3 collective-permute-start.4
  94.1 3.9 collective-permute-start.5
  98.1 6.3 collective-permute-start.6
  99.4 6.8 collective-permute-start.7
  129.9 94.3 %copy-start.2 = (f32[96,81,32]{1,0,2:T(8,128)S(1)}, f32[96,81,32]{1,0,2:T(8,128)}, u32[]{:S(2)}) copy-start(f32[96,81,32]{1,0,2:T(8,128)} %copy-done.1) | copy-start | bytes 2985988
  245.1 4.3 collective-permute-start.8
  246.4 3.9 collective-permute-start.9
  250.3 6.0 collective-permute-start.10
  251.6 6.4 collective-permute-start.11
  281.8 91.7 %copy-start.3 = (f32[96,81,32]{1,0,2:T(8,128)S(1)}, f32[96,81,32]{1,0,2:T(8,128)}, u32[]{:S(2)}) copy-start(f32[96,81,32]{1,0,2:T(8,128)} %copy-done.1) | copy-start | bytes 2985988
  394.4 4.3 collective-permute-start.12
  395.7 3.9 collective-permute-start.13
  399.7 6.0 collective-permute-start.14
  401.0 6.4 collective-permute-start.15
  431.2 92.3 %copy-start.4 = (f32[96,81,32]{1,0,2:T(8,128)S(1)}, f32[96,81,32]{1,0,2:T(8,128)}, u32[]{:S(2)}) copy-start(f32[96,81,32]{1,0,2:T(8,128)} %copy-done.1) | copy-start | bytes 2985988
  544.3 4.3 collective-permute-start.16
  545.6 3.9 collective-permute-start.17
  549.6 6.0 collective-permute-start.18
  550.9 6.4 collective-permute-start.19
  581.1 49.6 %copy-start.5 = (f32[96,81,32]{1,0,2:T(8,128)S(1)}, f32[96,81,32]{1,0,2:T(8,128)}, u32[]{:S(2)}) copy-start(f32[96,81,32]{1,0,2:T(8,128)} %copy-done.1) | copy-start | bytes 2985988
  655.7 9.5 %collective-permute-start.20 = (f32[3,1,32,128]{3,2,1,0:T(8,128)S(1)}, f32[3,1,32,128]{3,2,1,0:T(8,128)S(1)}, u32[]{:S(2)}, u32[]{:S(2)}) collective-permute-start(f32[3,1,32,128]{3,2,1,0:T(8,128)S(1)} %get-tuple-element.23), channel_id=1, source_target_pairs={{4,0},{8,4},{12,8},{16,12},{20,16},{24,20},{28,24},{5,1},{9,5},{13... | collective-permute-start | bytes 147464 | tf_op jit(solution)/shard_map/ppermute | solution.py:22
  657.0 8.2 %collective-permute-start.21 = (f32[3,1,32,128]{3,2,1,0:T(8,128)S(1)}, f32[3,1,32,128]{3,2,1,0:T(8,128)S(1)}, u32[]{:S(2)}, u32[]{:S(2)}) collective-permute-start(f32[3,1,32,128]{3,2,1,0:T(8,128)S(1)} %get-tuple-element.22), channel_id=1, source_target_pairs={{0,4},{4,8},{8,12},{12,16},{16,20},{20,24},{24,28},{1,5},{5,9},{9,... | collective-permute-start | bytes 147464 | tf_op jit(solution)/shard_map/ppermute | solution.py:20
  660.0 11.1 %all-to-all-start.3 = ((f32[81,8,4]{0,2,1:T(4,128)}), f32[81,8,4]{0,2,1:T(4,128)S(1)}, u32[]{:S(2)}, u32[]{:S(2)}) async-start(f32[81,8,4]{0,2,1:T(4,128)} %bitcast.55), calls=%async_computation.3 | async-start | bytes 32768 | tf_op jit(solution)/shard_map/all_to_all | solution.py:110
  665.3 7.1 %collective-permute-start.22 = (f32[3,34,1,128]{3,2,1,0:T(1,128)S(1)}, f32[3,34,1,128]{3,2,1,0:T(1,128)S(1)}, u32[]{:S(2)}, u32[]{:S(2)}) collective-permute-start(f32[3,34,1,128]{3,2,1,0:T(1,128)S(1)} %get-tuple-element.11), channel_id=1, source_target_pairs={{1,0},{2,1},{3,2},{5,4},{6,5},{7,6},{9,8},{10,9},{11,10},{13,12},{... | collective-permute-start | bytes 156680 | tf_op jit(solution)/shard_map/ppermute | solution.py:22
  666.6 6.3 collective-permute-start.23
  (16 other events, 122.5 us)
where the time goes:
time: 687 us; the launch traced here: 680 us
  blocking collectives  301 us (44%)
  other arithmetic  141 us (21%)
  local copies, waits for them, and re-layouts  106 us (15%)
  starting transfers between devices  81.8 us (12%)
  matrix products  26.5 us (4%)
  waiting for transfers between devices  12.8 us (2%)
  between operations  11 us (2%)
    psum x4, blocking collectives, total_squares(): return lax.psum(jnp.sum(residual * residual), ('gx', 'gy'))  170 us
    psum x3, blocking collectives, shards(): step_size = norm_now / lax.psum(jnp.sum(direction * image), ('gx', 'gy'))  132 us
    gather x15, local copies, waits for them, and re-layouts, collect(): return fluid_field.reshape(-1)[dof_index]  87.7 us
    scatter-add x5, other arithmetic, spread(): flat = jnp.zeros((COMP * cell_total,), jnp.float32).at[dof_index.reshape(...  85.6 us
    ppermute x12, starting transfers between devices, padded_2(): lax.ppermute(tail, axis, [(i, (i + 1) % count) for i in range(ends)])  46.4 us
    concatenate x12, other arithmetic, padded_2(): jnp.concatenate([lax.ppermute(tail, axis, [(i, (i + 1) % count) for i in...  22 us
    add x6, other arithmetic, smooth(): first_pass + (residual_in - operate(first_pass, shift_coef)) / diagonal  20 us
    ppermute x12, starting transfers between devices, padded_2(): lax.ppermute(head, axis, [((i + 1) % count, i) for i in range(ends)])  15.5 us
  transfers between devices with their start and end apart: 28, of which 11 were waited for; matrix products, arithmetic and copies ran while one was open for 6% of the time, Pallas kernels for 0%

commit v1 on v0

v1 whole, which is shorter than its diff:
```python
import functools
import jax
import jax.numpy as jnp
from jax import lax
from jax.experimental import pallas as pl
from jax.experimental.pallas import tpu as pltpu
from jax.sharding import PartitionSpec as P

COMP = 3
NODES = 32
MULT = 81
ITERS = 4
CAP = 4
ROWS = 88
MESH = pl.DeviceIdType.MESH


def pieces(values):
    high = values.astype(jnp.bfloat16).astype(jnp.float32)
    return jnp.concatenate([high, values - high], axis=0).astype(jnp.bfloat16)


def uzawa_kernel(ngx, ngy, slots, strides, spans, row_ref, col_ref, inv_ref, block_ref, goal_ref,
                 mult_ref, out_ref, links, sent, got, part, line, total, far, swap_sem, line_sem, far_sem):
    me_x, me_y = lax.axis_index("gx"), lax.axis_index("gy")
    nodes = row_ref.shape[1]
    quads = nodes // 128
    z_step, x_step = strides
    x_span, y_span = spans

    barrier = pltpu.get_barrier_semaphore()
    for o in range(1, ngx):
        pl.semaphore_signal(barrier, inc=1, device_id={"gx": lax.rem(me_x + o, ngx)}, device_id_type=MESH)
    for o in range(1, ngy):
        pl.semaphore_signal(barrier, inc=1, device_id={"gy": lax.rem(me_y + o, ngy)}, device_id_type=MESH)
    pl.semaphore_wait(barrier, ngx + ngy - 2)

    def exchange(source, slot):
        copies = []
        for side, (axis, me, count, step) in enumerate(
            (("gx", me_x, ngx, 1), ("gx", me_x, ngx, ngx - 1), ("gy", me_y, ngy, 1), ("gy", me_y, ngy, ngy - 1))
        ):
            copy = pltpu.make_async_remote_copy(
                src_ref=source, dst_ref=got.at[slot, side],
                send_sem=swap_sem.at[0, slot, side], recv_sem=swap_sem.at[1, slot, side],
                device_id={axis: lax.rem(me + step, count)}, device_id_type=MESH)
            copy.start()
            copies.append(copy)
        return copies

    copies = exchange(row_ref, 0)
    tile = 128

    @pl.loop(0, nodes // tile)
    def _(i):
        at = pl.ds(pl.multiple_of(i * tile, tile), tile)
        gap = jnp.abs(row_ref[0:1, :] - col_ref[at, :])
        links[0, at, :] = jnp.where(gap == 0.0, 1.0, 0.0).astype(jnp.bfloat16)
        links[1, at, :] = jnp.where(
            (gap == 1.0) | (gap == z_step) | (gap == x_step), 1.0, 0.0).astype(jnp.bfloat16)

    for copy in copies:
        copy.wait()
    nowhere = jnp.float32(8.0 * (x_span + x_step))
    from_left = jnp.where(me_x > 0, x_step - x_span, nowhere).astype(jnp.float32)
    from_right = jnp.where(me_x < ngx - 1, x_span - x_step, nowhere).astype(jnp.float32)
    from_below = jnp.where(me_y > 0, z_step - y_span, nowhere).astype(jnp.float32)
    from_above = jnp.where(me_y < ngy - 1, y_span - z_step, nowhere).astype(jnp.float32)

    @pl.loop(0, nodes // tile)
    def _(i):
        at = pl.ds(pl.multiple_of(i * tile, tile), tile)
        own = col_ref[at, :]
        for side, offset in enumerate((from_left, from_right, from_below, from_above)):
            moved = got[0, side, 0:1, :] + offset
            links[2 + side, at, :] = jnp.where(moved == own, 1.0, 0.0).astype(jnp.bfloat16)

    def apply_link(kind, values):
        both = lax.dot_general(
            pieces(values), links[kind], (((1,), (1,)), ((), ())), preferred_element_type=jnp.float32)
        return both[0:8] + both[8:16]

    def apply_bt(multi, into):
        for c in range(COMP):
            for q in range(quads):
                into[c:c + 1, q * 128:(q + 1) * 128] = jnp.sum(
                    block_ref[c * quads + q] * multi, axis=0, keepdims=True)

    def apply_b(values):
        image = jnp.zeros((ROWS, 128), jnp.float32)
        for c in range(COMP):
            for q in range(quads):
                image = image + block_ref[c * quads + q] * values[c:c + 1, q * 128:(q + 1) * 128]
        shift = 64
        while shift >= slots:
            image = image + pltpu.roll(image, shift, 1)
            shift //= 2
        return image

    def all_sum(slot):
        for axis, me, count, source, room, sems in (
            ("gx", me_x, ngx, part, line, line_sem), ("gy", me_y, ngy, total, far, far_sem)):
            copies = []
            for o in range(1, count):
                copy = pltpu.make_async_remote_copy(
                    src_ref=source, dst_ref=room.at[slot, o],
                    send_sem=sems.at[0, slot, o], recv_sem=sems.at[1, slot, o],
                    device_id={axis: lax.rem(me + o, count)}, device_id_type=MESH)
                copy.start()
                copies.append(copy)
            summed = source[...]
            for o, copy in enumerate(copies):
                copy.wait()
                summed = summed + room[slot, o + 1]
            if axis == "gx":
                total[...] = summed
        return summed

    sent[...] = jnp.zeros_like(sent)
    part[...] = jnp.zeros_like(part)
    inverse = inv_ref[...]

    def step(iteration, state):
        multi, residual, direction = state
        apply_bt(direction, sent)
        scaled = sent[...] * inverse
        sent[...] = scaled
        copies = exchange(sent, iteration + 1)
        here = apply_link(0, scaled)
        beside = apply_link(1, scaled)
        for side, copy in enumerate(copies):
            copy.wait()
            beside = beside + apply_link(2 + side, got[iteration + 1, side])
        image = apply_b(here + beside * inverse)
        for row, (a, b) in enumerate(
            ((residual, residual), (direction, image), (residual, image), (image, image))):
            part[row:row + 1, :] = jnp.sum(a * b, axis=0, keepdims=True)
        sums = jnp.sum(all_sum(iteration), axis=1, keepdims=True)
        norm_now, bend, cross, square = sums[0:1], sums[1:2], sums[2:3], sums[3:4]
        step_size = norm_now / bend
        norm_next = norm_now - 2.0 * step_size * cross + step_size * step_size * square
        multi = multi + step_size * direction
        residual = residual - step_size * image
        direction = residual + norm_next / norm_now * direction
        return multi, residual, direction

    goal = goal_ref[...]
    multi, _, _ = lax.fori_loop(0, ITERS, step, (jnp.zeros_like(goal), goal, goal))
    mult_ref[...] = multi
    out_ref[...] = jnp.zeros_like(out_ref)
    apply_bt(multi, out_ref)


def smooth(residual_in, shift_coef):
    inverse = 1.0 / (6.0 + shift_coef)
    first_pass = residual_in * inverse
    count_x, count_y = lax.axis_size("gx"), lax.axis_size("gy")

    def halo(axis, dim, count):
        head = lax.slice_in_dim(first_pass, 0, 1, axis=dim)
        tail = lax.slice_in_dim(first_pass, first_pass.shape[dim] - 1, first_pass.shape[dim], axis=dim)
        before = lax.ppermute(tail, axis, [(i, i + 1) for i in range(count - 1)])
        after = lax.ppermute(head, axis, [(i + 1, i) for i in range(count - 1)])
        grown = jnp.concatenate([before, first_pass, after], axis=dim)
        size = first_pass.shape[dim]
        return lax.slice_in_dim(grown, 0, size, axis=dim) + lax.slice_in_dim(grown, 2, size + 2, axis=dim)

    beside = halo("gx", 1, count_x) + halo("gy", 2, count_y)
    wide = jnp.pad(first_pass, ((0, 0), (0, 0), (0, 0), (1, 1)))
    beside = beside + wide[..., 2:] + wide[..., :-2]
    return first_pass + beside * inverse


def shards(body_force, shift_coef, coupling, node_cells, target_gap, new_owner):
    groups, rows_gy = lax.axis_size("gx"), lax.axis_size("gy")
    slots = groups * CAP
    pack = 128 // slots
    quads = NODES // pack
    nodes = NODES * slots
    owners = new_owner[:, 0]
    onehot = (owners[:, None] == jnp.arange(groups, dtype=jnp.int32)[None, :]).astype(jnp.int32)
    rank_in = jnp.sum((jnp.cumsum(onehot, axis=0) - 1) * onehot, axis=1)
    slot_of = owners * CAP + rank_in
    _, cx, cy, cz = body_force.shape
    cell_total = cx * cy * cz

    held = jnp.concatenate([coupling, node_cells.astype(jnp.float32), target_gap], axis=0)
    choose = (slot_of[:, None] == jnp.arange(slots, dtype=jnp.int32)[None, :]).astype(jnp.float32)
    held = jnp.dot(held, choose, precision=lax.Precision.HIGHEST)
    moved = lax.all_to_all(held, "gx", split_axis=1, concat_axis=1, tiled=True)
    block_rows = COMP * NODES * MULT
    blocks = moved[:block_rows].reshape(COMP * quads, pack, MULT, slots)
    blocks = jnp.pad(blocks.transpose(0, 2, 1, 3).reshape(COMP * quads, MULT, 128), ((0, 0), (0, ROWS - MULT), (0, 0)))
    cell_int = jnp.round(moved[block_rows:block_rows + NODES]).astype(jnp.int32).reshape(nodes)
    gap = moved[block_rows + NODES:]

    z_step = cz + 2
    x_step = z_step * (3 * cy + 4)
    ids = (cell_int // (cy * cz) * x_step + cell_int // cz % cy * z_step + cell_int % cz).astype(jnp.float32)
    dof_index = jnp.arange(COMP, dtype=jnp.int32)[:, None] * cell_total + cell_int[None]
    start = smooth(body_force, shift_coef).reshape(-1)[dof_index].reshape(COMP * quads, 128)
    image = jnp.sum(blocks * start[:, None, :], axis=0)
    image = jnp.sum(image.reshape(ROWS, pack, slots), axis=1)
    goal = jnp.tile(image - jnp.pad(gap, ((0, ROWS - MULT), (0, 0))), (1, pack))
    inverse = 1.0 / (6.0 + shift_coef.reshape(-1)[cell_int])

    vmem = pl.BlockSpec(memory_space=pltpu.VMEM)
    multi, force = pl.pallas_call(
        functools.partial(
            uzawa_kernel, groups, rows_gy, slots, (float(z_step), float(x_step)),
            (float(cx * x_step), float(cy * z_step))),
        out_shape=(
            jax.ShapeDtypeStruct((ROWS, 128), jnp.float32),
            jax.ShapeDtypeStruct((8, nodes), jnp.float32),
        ),
        in_specs=[vmem] * 5,
        out_specs=(vmem, vmem),
        scratch_shapes=[
            pltpu.VMEM((6, nodes, nodes), jnp.bfloat16),
            pltpu.VMEM((8, nodes), jnp.float32),
            pltpu.VMEM((ITERS + 1, 4, 8, nodes), jnp.float32),
            pltpu.VMEM((8, 128), jnp.float32),
            pltpu.VMEM((ITERS, groups, 8, 128), jnp.float32),
            pltpu.VMEM((8, 128), jnp.float32),
            pltpu.VMEM((ITERS, rows_gy, 8, 128), jnp.float32),
            pltpu.SemaphoreType.DMA((2, ITERS + 1, 4)),
            pltpu.SemaphoreType.DMA((2, ITERS, groups)),
            pltpu.SemaphoreType.DMA((2, ITERS, rows_gy)),
        ],
        compiler_params=pltpu.CompilerParams(
            collective_id=0, has_side_effects=True,
            vmem_limit_bytes=(12 * nodes * nodes + (12 << 20))),
    )(
        jnp.broadcast_to(ids[None], (8, nodes)), ids[:, None],
        jnp.broadcast_to(inverse[None], (8, nodes)), blocks, goal,
    )

    flat = jnp.zeros((COMP * cell_total,), jnp.float32).at[dof_index.reshape(-1)].add(force[:COMP].reshape(-1))
    velocity = smooth(body_force - flat.reshape(body_force.shape), shift_coef)
    back = lax.all_to_all(multi[:MULT, :slots], "gx", split_axis=1, concat_axis=1, tiled=True)
    multipliers = jnp.dot(back, choose.T, precision=lax.Precision.HIGHEST)
    return (multipliers, velocity)


def solution(mesh):
    in_specs = (
        P(None, "gx", "gy", None),
        P("gx", "gy", None),
        P(None, ("gx", "gy")),
        P(None, ("gx", "gy")),
        P(None, ("gx", "gy")),
        P(("gx", "gy"), None),
    )
    out_specs = (P(None, ("gx", "gy")), P(None, "gx", "gy", None))
    return jax.shard_map(shards, mesh=mesh, in_specs=in_specs, out_specs=out_specs, check_vma=False)
```

time: 687 us -> 172 us (0.25)
  blocking collectives: 301 us -> 0 us
  other arithmetic: 141 us -> 29 us
  local copies, waits for them, and re-layouts: 106 us -> 42.7 us
  Pallas kernels: 0 us -> 61.9 us
  starting transfers between devices: 81.8 us -> 24.9 us
  matrix products: 26.5 us -> 1.48 us
  between operations: 11 us -> 0.97 us
    psum x7 -> x0, blocking collectives: 301 us -> none  [the longest x4 170 us: total_squares(): return lax.psum(jnp.sum(residual * residual), ('gx', 'gy'))]
    scatter-add x5 -> x1, other arithmetic: 85.6 us -> 17.8 us  [shards(): jnp.zeros((COMP * cell_total,), jnp.float32).at[dof_index.reshape(-1)]]
    gather x16 -> x2, local copies, waits for them, and re-layouts: 88.9 us -> 23.6 us  [the longest x1 17.4 us: shards(): smooth(body_force, shift_coef).reshape(-1)[dof_index]]
    pallas_call x0 -> x1, Pallas kernels: none -> 61.9 us  [shards(): pl.pallas_call(functools.partial(uzawa_kernel, groups, rows_gy, slots, (f...]
    ppermute x24 -> x8, starting transfers between devices: 61.8 us -> 16.3 us  [the longest x4 11.1 us: halo(): before = lax.ppermute(tail, axis, [(i, i + 1) for i in range(count - 1)])]
    dot_general x10 -> x2, matrix products: 26.5 us -> 1.48 us  [the longest x1 0.81 us: shards(): multipliers = jnp.dot(back, choose.T, precision=lax.Precision.HIGHEST)]
    concatenate x12 -> x0, other arithmetic: 22 us -> none  [padded_2(): jnp.concatenate([lax.ppermute(tail, axis, [(i, (i + 1) % count) for i in...]
    add x12 -> x2, other arithmetic: 21.9 us -> 3.02 us  [smooth(): return first_pass + beside * inverse]
  transfers between devices with their start and end apart: 28 -> 10, of which waited for: 11 -> 4; matrix products, arithmetic and copies ran while one was open for 6% -> 1% of each run, Pallas kernels for 0% -> 0%
where the time goes in v1:
time: 172 us; the launch traced here: 170 us
  Pallas kernels  61.9 us (36%)
  local copies, waits for them, and re-layouts  42.7 us (25%)
  other arithmetic  29 us (17%)
  starting transfers between devices  24.9 us (14%)
  waiting for transfers between devices  8.68 us (5%)
    pallas_call x1, Pallas kernels, shards(): pl.pallas_call(functools.partial(uzawa_kernel, groups, rows_gy, slots, (f...  61.9 us
    scatter-add x1, other arithmetic, shards(): jnp.zeros((COMP * cell_total,), jnp.float32).at[dof_index.reshape(-1)]  17.8 us
    gather x1, local copies, waits for them, and re-layouts, shards(): smooth(body_force, shift_coef).reshape(-1)[dof_index]  17.4 us
    ppermute x4, starting transfers between devices, halo(): before = lax.ppermute(tail, axis, [(i, i + 1) for i in range(count - 1)])  11.1 us
    ppermute x4, waiting for transfers between devices, halo(): after = lax.ppermute(head, axis, [(i + 1, i) for i in range(count - 1)])  8.11 us
    gather x1, local copies, waits for them, and re-layouts, shards(): inverse = 1.0 / (6.0 + shift_coef.reshape(-1)[cell_int])  6.15 us
    all_to_all x1, starting transfers between devices, shards(): moved = lax.all_to_all(held, 'gx', split_axis=1, concat_axis=1, tiled=True)  5.3 us
    ppermute x4, starting transfers between devices, halo(): after = lax.ppermute(head, axis, [(i + 1, i) for i in range(count - 1)])  5.17 us
  transfers between devices with their start and end apart: 10, of which 4 were waited for; matrix products, arithmetic and copies ran while one was open for 1% of the time, Pallas kernels for 0%

profile of v1, /device:TPU:0, one launch (start us, length us, event | category | flops | bytes accessed | tf_op | source)
XLA Modules:
  0.0 169.7 jit_solution(9341500175936195273)
XLA Ops:
  0.6 0.7 fusion.29
  1.4 0.8 select_reduce_fusion
  3.7 1.3 concatenate.31
  5.7 1.2 all_to_all.14
  6.9 5.3 %all-to-all-start = ((f32[7889,8,4]{0,2,1:T(4,128)}), f32[7889,8,4]{0,2,1:T(4,128)}, u32[]{:S(2)}, u32[]{:S(2)}) async-start(f32[7889,8,4]{0,2,1:T(4,128)} %all_to_all.14), calls=%async_computation | async-start | bytes 2031616 | tf_op jit(solution)/shard_map/all_to_all | solution.py:190
  12.6 2.4 %collective-permute-start = (f32[3,1,32,128]{3,2,1,0:T(8,128)S(1)}, f32[3,1,32,128]{3,2,1,0:T(8,128)S(1)}, u32[]{:S(2)}, u32[]{:S(2)}) collective-permute-start(f32[3,1,32,128]{3,2,1,0:T(8,128)S(1)} %get-tuple-element.10), channel_id=1, source_target_pairs={{0,4},{4,8},{8,12},{12,16},{16,20},{20,24},{24,28},{1,5},{5,9},{9,... | collective-permute-start | bytes 147464 | tf_op jit(solution)/shard_map/ppermute | solution.py:162
  15.0 1.3 collective-permute-start.1
  16.4 3.9 %collective-permute-start.2 = (f32[3,32,1,128]{3,2,1,0:T(1,128)S(1)}, f32[3,32,1,128]{3,2,1,0:T(1,128)S(1)}, u32[]{:S(2)}, u32[]{:S(2)}) collective-permute-start(f32[3,32,1,128]{3,2,1,0:T(1,128)S(1)} %get-tuple-element.12), channel_id=1, source_target_pairs={{0,1},{1,2},{2,3},{4,5},{5,6},{6,7},{8,9},{9,10},{10,11},{12,13},{... | collective-permute-start | bytes 147464 | tf_op jit(solution)/shard_map/ppermute | solution.py:162
  20.3 1.3 collective-permute-start.3
  22.0 4.3 %collective-permute-done.3 = f32[3,32,1,128]{3,2,1,0:T(1,128)S(1)} collective-permute-done((f32[3,32,1,128]{3,2,1,0:T(1,128)S(1)}, f32[3,32,1,128]{3,2,1,0:T(1,128)S(1)}, u32[]{:S(2)}, u32[]{:S(2)}) %collective-permute-start.3) | collective-permute-done | bytes 49184 | tf_op jit(solution)/shard_map/ppermute | solution.py:163
  26.2 1.0 fusion.3
  27.4 0.8 slice.118
  28.9 2.2 %slice.119 = f32[7776,8,4]{0,2,1:T(4,128)} slice(f32[7889,8,4]{0,2,1:T(4,128)} %all-to-all-done), slice={[0:7776], [0:8], [0:4]} | slice | bytes 1990656 | tf_op jit(solution)/shard_map/slice | solution.py:192
  31.1 4.9 %reshape.408 = f32[24,4,81,32]{2,1,0,3:T(4,128)} reshape(f32[7776,8,4]{0,2,1:T(4,128)} %slice.119) | data formatting | bytes 1990656 | tf_op jit(solution)/shard_map/reshape | solution.py:192
  36.0 3.5 %copy.83 = f32[24,81,4,32]{1,3,2,0:T(8,128)} copy(f32[24,81,4,32]{1,2,0,3:T(4,128)} %bitcast.36) | data formatting | bytes 1990656 | tf_op jit(solution)/shard_map/transpose | solution.py:193
  39.5 2.9 %copy.84 = f32[24,81,128]{2,1,0:T(8,128)} copy(f32[24,81,128]{1,2,0:T(8,128)} %bitcast.38) | data formatting | bytes 1990656 | tf_op jit(solution)/shard_map/reshape | solution.py:193
  42.4 17.4 %gather_fusion.1 = f32[3072]{0:T(1024)S(1)} fusion(f32[393216]{0:T(1024)S(1)} %bitcast.34, s32[3072]{0:T(1024)S(1)} %broadcast_clamp_fusion), kind=kCustom, calls=%fused_computation.1 | custom fusion | bytes 36864 | tf_op jit(solution)/shard_map/gather | solution.py:201
  59.8 1.4 multiply_reduce_fusion
  61.3 0.7 slice.124
  62.1 1.0 fusion.23
  63.2 6.2 %gather_fusion = f32[1024]{0:T(1024)S(1)} fusion(f32[131072]{0:T(1024)S(1)} %bitcast.35, s32[1024]{0:T(1024)S(1)} %broadcast_clamp_fusion.1), kind=kCustom, calls=%fused_computation | custom fusion | bytes 12288 | tf_op jit(solution)/shard_map/gather | solution.py:205
  69.4 61.9 %shard_map.77 = (f32[88,128]{1,0:T(8,128)S(1)}, f32[8,1024]{1,0:T(8,128)S(1)}) custom-call(f32[8,1024]{1,0:T(8,128)S(1)} %broadcast_in_dim.6.row_ref, f32[1024,1]{1,0:T(8,128)S(1)} %get-tuple-element.17.col_ref, f32[8,1024]{1,0:T(8,128)S(1)} %broadcast_in_dim.7.inv_ref, f32[24,88,128]{2,1,0:T(8,128)S(1)} %get-tuple-element.15.block_ref, ...), custom_call_target="tpu_custom_call" | custom-call | tf_op jit(solution)/shard_map/pallas_call | solution.py:208
  131.3 17.8 %scatter_custom_fusion = f32[393216]{0:T(1024)} fusion(s32[3072]{0:T(1024)S(1)} %bitcast.45, f32[3072]{0:T(1024)S(1)} %reshape.434, f32[]{:T(128)} %constant.84.clone.1), kind=kCustom, calls=%fused_computation.31 | custom fusion | flops 3072 | bytes 1572868 | tf_op jit(solution)/shard_map/scatter-add | solution.py:238
  149.1 2.3 %subtract_multiply_fusion = f32[3,32,32,128]{3,2,1,0:T(8,128)S(1)} fusion(f32[3,32,32,128]{3,2,1,0:T(8,128)} %param.6, f32[3,32,32,128]{3,2,1,0:T(8,128)} %bitcast.37, f32[32,32,128]{2,1,0:T(8,128)S(1)} %add_divide_fusion), kind=kLoop, calls=%fused_computation.29 | loop fusion | flops 786432 | bytes 5242880 | tf_op jit(solution)/shard_map/mul | solution.py:156
  152.2 3.3 %all-to-all-start.1 = ((f32[81,8,4]{0,2,1:T(4,128)}), f32[81,8,4]{0,2,1:T(4,128)S(1)}, u32[]{:S(2)}, u32[]{:S(2)}) async-start(f32[81,8,4]{0,2,1:T(4,128)} %bitcast.11), calls=%async_computation.1 | async-start | bytes 32768 | tf_op jit(solution)/shard_map/all_to_all | solution.py:240
  155.5 2.3 %collective-permute-start.4 = (f32[3,1,32,128]{3,2,1,0:T(8,128)S(1)}, f32[3,1,32,128]{3,2,1,0:T(8,128)S(1)}, u32[]{:S(2)}, u32[]{:S(2)}) collective-permute-start(f32[3,1,32,128]{3,2,1,0:T(8,128)S(1)} %get-tuple-element.6), channel_id=1, source_target_pairs={{0,4},{4,8},{8,12},{12,16},{16,20},{20,24},{24,28},{1,5},{5,9},{9,... | collective-permute-start | bytes 147464 | tf_op jit(solution)/shard_map/ppermute | solution.py:162
  157.9 1.3 collective-permute-start.5
  159.2 2.5 %collective-permute-start.6 = (f32[3,32,1,128]{3,2,1,0:T(1,128)S(1)}, f32[3,32,1,128]{3,2,1,0:T(1,128)S(1)}, u32[]{:S(2)}, u32[]{:S(2)}) collective-permute-start(f32[3,32,1,128]{3,2,1,0:T(1,128)S(1)} %get-tuple-element.8), channel_id=1, source_target_pairs={{0,1},{1,2},{2,3},{4,5},{5,6},{6,7},{8,9},{9,10},{10,11},{12,13},{... | collective-permute-start | bytes 147464 | tf_op jit(solution)/shard_map/ppermute | solution.py:162
  161.7 1.3 collective-permute-start.7
  163.0 0.8 fusion.27
  163.8 3.9 %collective-permute-done.7 = f32[3,32,1,128]{3,2,1,0:T(1,128)S(1)} collective-permute-done((f32[3,32,1,128]{3,2,1,0:T(1,128)S(1)}, f32[3,32,1,128]{3,2,1,0:T(1,128)S(1)}, u32[]{:S(2)}, u32[]{:S(2)}) %collective-permute-start.7) | collective-permute-done | bytes 49184 | tf_op jit(solution)/shard_map/ppermute | solution.py:163
  167.7 2.0 %fusion.7 = f32[3,32,32,128]{3,2,1,0:T(8,128)} fusion(f32[3,32,32,128]{3,2,1,0:T(8,128)S(1)} %subtract_multiply_fusion, f32[3,32,1,128]{3,2,1,0:T(1,128)S(1)} %collective-permute-done.7, f32[3,32,1,128]{3,2,1,0:T(1,128)S(1)} %collective-permute-done.6, f32[3,1,32,128]{3,2,1,0:T(8,128)S(1)} %collective-permute-done.5, ...), kind=kLoop, calls=%fused_computation.14 | loop fusion | flops 4325376 | bytes 3866624 | tf_op jit(solution)/shard_map/add | solution.py:171
  (47 shorter events, 4.8 us)
Async XLA Ops:
  5.7 6.6 %copy-start = (f32[32,32,128]{2,1,0:T(8,128)S(1)}, f32[32,32,128]{2,1,0:T(8,128)}, u32[]{:S(2)}) copy-start(f32[32,32,128]{2,1,0:T(8,128)} %param.7) | copy-start | bytes 1572868
  6.9 5.4 %copy-start.1 = (f32[3,32,32,128]{3,2,1,0:T(8,128)S(1)}, f32[3,32,32,128]{3,2,1,0:T(8,128)}, u32[]{:S(2)}) copy-start(f32[3,32,32,128]{3,2,1,0:T(8,128)} %param.6) | copy-start | bytes 4718596
  6.9 20.5 %all-to-all-start = ((f32[7889,8,4]{0,2,1:T(4,128)}), f32[7889,8,4]{0,2,1:T(4,128)}, u32[]{:S(2)}, u32[]{:S(2)}) async-start(f32[7889,8,4]{0,2,1:T(4,128)} %all_to_all.14), calls=%async_computation | async-start | bytes 2031616 | tf_op jit(solution)/shard_map/all_to_all | solution.py:190
  12.6 9.0 %collective-permute-start = (f32[3,1,32,128]{3,2,1,0:T(8,128)S(1)}, f32[3,1,32,128]{3,2,1,0:T(8,128)S(1)}, u32[]{:S(2)}, u32[]{:S(2)}) collective-permute-start(f32[3,1,32,128]{3,2,1,0:T(8,128)S(1)} %get-tuple-element.10), channel_id=1, source_target_pairs={{0,4},{4,8},{8,12},{12,16},{16,20},{20,24},{24,28},{1,5},{5,9},{9,... | collective-permute-start | bytes 147464 | tf_op jit(solution)/shard_map/ppermute | solution.py:162
  15.0 6.6 %collective-permute-start.1 = (f32[3,1,32,128]{3,2,1,0:T(8,128)S(1)}, f32[3,1,32,128]{3,2,1,0:T(8,128)S(1)}, u32[]{:S(2)}, u32[]{:S(2)}) collective-permute-start(f32[3,1,32,128]{3,2,1,0:T(8,128)S(1)} %get-tuple-element.11), channel_id=1, source_target_pairs={{4,0},{8,4},{12,8},{16,12},{20,16},{24,20},{28,24},{5,1},{9,5},{13... | collective-permute-start | bytes 147464 | tf_op jit(solution)/shard_map/ppermute | solution.py:163
  16.4 5.6 %collective-permute-start.2 = (f32[3,32,1,128]{3,2,1,0:T(1,128)S(1)}, f32[3,32,1,128]{3,2,1,0:T(1,128)S(1)}, u32[]{:S(2)}, u32[]{:S(2)}) collective-permute-start(f32[3,32,1,128]{3,2,1,0:T(1,128)S(1)} %get-tuple-element.12), channel_id=1, source_target_pairs={{0,1},{1,2},{2,3},{4,5},{5,6},{6,7},{8,9},{9,10},{10,11},{12,13},{... | collective-permute-start | bytes 147464 | tf_op jit(solution)/shard_map/ppermute | solution.py:162
  20.3 6.0 %collective-permute-start.3 = (f32[3,32,1,128]{3,2,1,0:T(1,128)S(1)}, f32[3,32,1,128]{3,2,1,0:T(1,128)S(1)}, u32[]{:S(2)}, u32[]{:S(2)}) collective-permute-start(f32[3,32,1,128]{3,2,1,0:T(1,128)S(1)} %get-tuple-element.13), channel_id=1, source_target_pairs={{1,0},{2,1},{3,2},{5,4},{6,5},{7,6},{9,8},{10,9},{11,10},{13,12},{... | collective-permute-start | bytes 147464 | tf_op jit(solution)/shard_map/ppermute | solution.py:163
  152.2 10.8 %all-to-all-start.1 = ((f32[81,8,4]{0,2,1:T(4,128)}), f32[81,8,4]{0,2,1:T(4,128)S(1)}, u32[]{:S(2)}, u32[]{:S(2)}) async-start(f32[81,8,4]{0,2,1:T(4,128)} %bitcast.11), calls=%async_computation.1 | async-start | bytes 32768 | tf_op jit(solution)/shard_map/all_to_all | solution.py:240
  155.5 8.2 %collective-permute-start.4 = (f32[3,1,32,128]{3,2,1,0:T(8,128)S(1)}, f32[3,1,32,128]{3,2,1,0:T(8,128)S(1)}, u32[]{:S(2)}, u32[]{:S(2)}) collective-permute-start(f32[3,1,32,128]{3,2,1,0:T(8,128)S(1)} %get-tuple-element.6), channel_id=1, source_target_pairs={{0,4},{4,8},{8,12},{12,16},{16,20},{20,24},{24,28},{1,5},{5,9},{9,... | collective-permute-start | bytes 147464 | tf_op jit(solution)/shard_map/ppermute | solution.py:162
  157.9 5.9 %collective-permute-start.5 = (f32[3,1,32,128]{3,2,1,0:T(8,128)S(1)}, f32[3,1,32,128]{3,2,1,0:T(8,128)S(1)}, u32[]{:S(2)}, u32[]{:S(2)}) collective-permute-start(f32[3,1,32,128]{3,2,1,0:T(8,128)S(1)} %get-tuple-element.7), channel_id=1, source_target_pairs={{4,0},{8,4},{12,8},{16,12},{20,16},{24,20},{28,24},{5,1},{9,5},{13... | collective-permute-start | bytes 147464 | tf_op jit(solution)/shard_map/ppermute | solution.py:163
  159.2 4.6 %collective-permute-start.6 = (f32[3,32,1,128]{3,2,1,0:T(1,128)S(1)}, f32[3,32,1,128]{3,2,1,0:T(1,128)S(1)}, u32[]{:S(2)}, u32[]{:S(2)}) collective-permute-start(f32[3,32,1,128]{3,2,1,0:T(1,128)S(1)} %get-tuple-element.8), channel_id=1, source_target_pairs={{0,1},{1,2},{2,3},{4,5},{5,6},{6,7},{8,9},{9,10},{10,11},{12,13},{... | collective-permute-start | bytes 147464 | tf_op jit(solution)/shard_map/ppermute | solution.py:162
  161.7 6.0 %collective-permute-start.7 = (f32[3,32,1,128]{3,2,1,0:T(1,128)S(1)}, f32[3,32,1,128]{3,2,1,0:T(1,128)S(1)}, u32[]{:S(2)}, u32[]{:S(2)}) collective-permute-start(f32[3,32,1,128]{3,2,1,0:T(1,128)S(1)} %get-tuple-element.9), channel_id=1, source_target_pairs={{1,0},{2,1},{3,2},{5,4},{6,5},{7,6},{9,8},{10,9},{11,10},{13,12},{... | collective-permute-start | bytes 147464 | tf_op jit(solution)/shard_map/ppermute | solution.py:163

commit v2 on v1

--- a/solution.py
+++ b/solution.py
@@ -20,8 +20,9 @@
     return jnp.concatenate([high, values - high], axis=0).astype(jnp.bfloat16)
 
 
-def uzawa_kernel(ngx, ngy, slots, strides, spans, row_ref, col_ref, inv_ref, block_ref, goal_ref,
-                 mult_ref, out_ref, links, sent, got, part, line, total, far, swap_sem, line_sem, far_sem):
+def uzawa_kernel(ngx, ngy, slots, strides, spans, force_ref, shift_ref, row_ref, col_ref,
+                 place_ref, block_ref, gap_ref, mult_ref, out_ref, links, inv, grown, edge, face, sent, got, part,
+                 line, total, far, face_sem, swap_sem, line_sem, far_sem):
     me_x, me_y = lax.axis_index("gx"), lax.axis_index("gy")
     nodes = row_ref.shape[1]
     quads = nodes // 128
@@ -48,8 +49,82 @@
             copies.append(copy)
         return copies
 
+    _, cx, cy, cz = force_ref.shape
+    columns = cx * cy
+    spot = links.shape[0] - 1
+
+    def start_faces(time):
+        for c in range(COMP):
+            edge[0, c] = grown[c, cx]
+            edge[1, c] = grown[c, 1]
+            edge[2, c] = grown[c, 1:cx + 1, cy - 1, :]
+            edge[3, c] = grown[c, 1:cx + 1, 0, :]
+        copies = []
+        for side, (axis, me, count, step) in enumerate(
+            (("gx", me_x, ngx, 1), ("gx", me_x, ngx, ngx - 1), ("gy", me_y, ngy, 1), ("gy", me_y, ngy, ngy - 1))
+        ):
+            copy = pltpu.make_async_remote_copy(
+                src_ref=edge.at[side], dst_ref=face.at[time, side],
+                send_sem=face_sem.at[0, time, side], recv_sem=face_sem.at[1, time, side],
+                device_id={axis: lax.rem(me + step, count)}, device_id_type=MESH)
+            copy.start()
+            copies.append(copy)
+        return copies
+
+    def finish_smooth(copies, time):
+        for copy in copies:
+            copy.wait()
+        for c in range(COMP):
+            grown[c, 0] = jnp.where(me_x > 0, face[time, 0, c], 0.0)
+            grown[c, cx + 1] = jnp.where(me_x < ngx - 1, face[time, 1, c], 0.0)
+        y_at = lax.broadcasted_iota(jnp.int32, (cy, cz), 0)
+        z_at = lax.broadcasted_iota(jnp.int32, (cy, cz), 1)
+
+        @pl.loop(0, cx)
+        def _(x):
+            scale = inv[x]
+            for c in range(COMP):
+                mid = grown[c, x + 1]
+                low = jnp.where(me_y > 0, face[time, 2, c, pl.ds(x, 1), :], 0.0)
+                high = jnp.where(me_y < ngy - 1, face[time, 3, c, pl.ds(x, 1), :], 0.0)
+                beside = grown[c, x] + grown[c, x + 2]
+                beside = beside + jnp.where(y_at == 0, low, pltpu.roll(mid, 1, 0))
+                beside = beside + jnp.where(y_at == cy - 1, high, pltpu.roll(mid, cy - 1, 0))
+                beside = beside + jnp.where(z_at == 0, 0.0, pltpu.roll(mid, 1, 1))
+                beside = beside + jnp.where(z_at == cz - 1, 0.0, pltpu.roll(mid, cz - 1, 1))
+                out_ref[c, x] = mid + beside * scale
+
+    def mark_spots():
+        @pl.loop(0, columns // 128)
+        def _(i):
+            at = pl.multiple_of(i * 128, 128)
+            here = lax.broadcasted_iota(jnp.int32, (128, nodes), 0) + at
+            links[spot, pl.ds(at, 128), :] = jnp.where(here == place_ref[0:1, :], 1.0, 0.0).astype(jnp.bfloat16)
+
+    def gather(field):
+        high = field.astype(jnp.bfloat16).astype(jnp.float32)
+        both = jnp.concatenate([high, field - high], axis=1).astype(jnp.bfloat16)
+        picked = lax.dot_general(
+            both, links[spot, 0:columns, :], (((0,), (0,)), ((), ())), preferred_element_type=jnp.float32)
+        z_row = lax.broadcasted_iota(jnp.int32, (cz, nodes), 0) == place_ref[1:2, :]
+        return jnp.sum(jnp.where(z_row, picked[:cz] + picked[cz:], 0.0), axis=0, keepdims=True)
+
+    def scatter(values):
+        high = values.astype(jnp.bfloat16).astype(jnp.float32)
+        z_row = lax.broadcasted_iota(jnp.int32, (cz, nodes), 0) == place_ref[1:2, :]
+        both = jnp.concatenate(
+            [jnp.where(z_row, high, 0.0), jnp.where(z_row, values - high, 0.0)], axis=0).astype(jnp.bfloat16)
+        summed = lax.dot_general(
+            links[spot, 0:columns, :], both, (((1,), (1,)), ((), ())), preferred_element_type=jnp.float32)
+        return (summed[:, :cz] + summed[:, cz:]).reshape(cx, cy, cz)
+
+    inv[...] = 1.0 / (6.0 + shift_ref[...])
+    for c in range(COMP):
+        grown[c, 1:cx + 1] = force_ref[c] * inv[...]
+    faces = start_faces(0)
     copies = exchange(row_ref, 0)
     tile = 128
+    mark_spots()
 
     @pl.loop(0, nodes // tile)
     def _(i):
@@ -58,6 +133,14 @@
         links[0, at, :] = jnp.where(gap == 0.0, 1.0, 0.0).astype(jnp.bfloat16)
         links[1, at, :] = jnp.where(
             (gap == 1.0) | (gap == z_step) | (gap == x_step), 1.0, 0.0).astype(jnp.bfloat16)
+
+    finish_smooth(faces, 0)
+    sent[...] = jnp.zeros_like(sent)
+    part[...] = jnp.zeros_like(part)
+    for c in range(COMP):
+        sent[c:c + 1, :] = gather(out_ref[c].reshape(columns, cz))
+    inverse = gather(inv[...].reshape(columns, cz))
+    start = sent[...]
 
     for copy in copies:
         copy.wait()
@@ -115,10 +198,6 @@
             if axis == "gx":
                 total[...] = summed
         return summed
-
-    sent[...] = jnp.zeros_like(sent)
-    part[...] = jnp.zeros_like(part)
-    inverse = inv_ref[...]
 
     def step(iteration, state):
         multi, residual, direction = state
@@ -144,31 +223,15 @@
         direction = residual + norm_next / norm_now * direction
         return multi, residual, direction
 
-    goal = goal_ref[...]
+    goal = apply_b(start) - gap_ref[...]
     multi, _, _ = lax.fori_loop(0, ITERS, step, (jnp.zeros_like(goal), goal, goal))
     mult_ref[...] = multi
-    out_ref[...] = jnp.zeros_like(out_ref)
-    apply_bt(multi, out_ref)
-
-
-def smooth(residual_in, shift_coef):
-    inverse = 1.0 / (6.0 + shift_coef)
-    first_pass = residual_in * inverse
-    count_x, count_y = lax.axis_size("gx"), lax.axis_size("gy")
-
-    def halo(axis, dim, count):
-        head = lax.slice_in_dim(first_pass, 0, 1, axis=dim)
-        tail = lax.slice_in_dim(first_pass, first_pass.shape[dim] - 1, first_pass.shape[dim], axis=dim)
-        before = lax.ppermute(tail, axis, [(i, i + 1) for i in range(count - 1)])
-        after = lax.ppermute(head, axis, [(i + 1, i) for i in range(count - 1)])
-        grown = jnp.concatenate([before, first_pass, after], axis=dim)
-        size = first_pass.shape[dim]
-        return lax.slice_in_dim(grown, 0, size, axis=dim) + lax.slice_in_dim(grown, 2, size + 2, axis=dim)
-
-    beside = halo("gx", 1, count_x) + halo("gy", 2, count_y)
-    wide = jnp.pad(first_pass, ((0, 0), (0, 0), (0, 0), (1, 1)))
-    beside = beside + wide[..., 2:] + wide[..., :-2]
-    return first_pass + beside * inverse
+    apply_bt(multi, sent)
+    if spot < 6:
+        mark_spots()
+    for c in range(COMP):
+        grown[c, 1:cx + 1] = (force_ref[c] - scatter(sent[c:c + 1, :])) * inv[...]
+    finish_smooth(start_faces(1), 1)
 
 
 def shards(body_force, shift_coef, coupling, node_cells, target_gap, new_owner):
@@ -197,46 +260,44 @@
     z_step = cz + 2
     x_step = z_step * (3 * cy + 4)
     ids = (cell_int // (cy * cz) * x_step + cell_int // cz % cy * z_step + cell_int % cz).astype(jnp.float32)
-    dof_index = jnp.arange(COMP, dtype=jnp.int32)[:, None] * cell_total + cell_int[None]
-    start = smooth(body_force, shift_coef).reshape(-1)[dof_index].reshape(COMP * quads, 128)
-    image = jnp.sum(blocks * start[:, None, :], axis=0)
-    image = jnp.sum(image.reshape(ROWS, pack, slots), axis=1)
-    goal = jnp.tile(image - jnp.pad(gap, ((0, ROWS - MULT), (0, 0))), (1, pack))
-    inverse = 1.0 / (6.0 + shift_coef.reshape(-1)[cell_int])
+    gap = jnp.tile(jnp.pad(gap, ((0, ROWS - MULT), (0, 0))), (1, pack))
+    place = jnp.pad(jnp.stack([cell_int // cz, cell_int % cz]), ((0, 6), (0, 0)))
 
     vmem = pl.BlockSpec(memory_space=pltpu.VMEM)
-    multi, force = pl.pallas_call(
+    multi, velocity = pl.pallas_call(
         functools.partial(
             uzawa_kernel, groups, rows_gy, slots, (float(z_step), float(x_step)),
             (float(cx * x_step), float(cy * z_step))),
         out_shape=(
             jax.ShapeDtypeStruct((ROWS, 128), jnp.float32),
-            jax.ShapeDtypeStruct((8, nodes), jnp.float32),
+            jax.ShapeDtypeStruct(body_force.shape, jnp.float32),
         ),
-        in_specs=[vmem] * 5,
+        in_specs=[vmem] * 7,
         out_specs=(vmem, vmem),
         scratch_shapes=[
-            pltpu.VMEM((6, nodes, nodes), jnp.bfloat16),
+            pltpu.VMEM((7 if nodes <= 1024 else 6, nodes, nodes), jnp.bfloat16),
+            pltpu.VMEM((cx, cy, cz), jnp.float32),
+            pltpu.VMEM((COMP, cx + 2, cy, cz), jnp.float32),
+            pltpu.VMEM((4, COMP, cy, cz), jnp.float32),
+            pltpu.VMEM((2, 4, COMP, cy, cz), jnp.float32),
             pltpu.VMEM((8, nodes), jnp.float32),
             pltpu.VMEM((ITERS + 1, 4, 8, nodes), jnp.float32),
             pltpu.VMEM((8, 128), jnp.float32),
             pltpu.VMEM((ITERS, groups, 8, 128), jnp.float32),
             pltpu.VMEM((8, 128), jnp.float32),
             pltpu.VMEM((ITERS, rows_gy, 8, 128), jnp.float32),
+            pltpu.SemaphoreType.DMA((2, 2, 4)),
             pltpu.SemaphoreType.DMA((2, ITERS + 1, 4)),
             pltpu.SemaphoreType.DMA((2, ITERS, groups)),
             pltpu.SemaphoreType.DMA((2, ITERS, rows_gy)),
         ],
         compiler_params=pltpu.CompilerParams(
             collective_id=0, has_side_effects=True,
-            vmem_limit_bytes=(12 * nodes * nodes + (12 << 20))),
+            vmem_limit_bytes=(46 << 20) if nodes <= 1024 else (63 << 20)),
     )(
-        jnp.broadcast_to(ids[None], (8, nodes)), ids[:, None],
-        jnp.broadcast_to(inverse[None], (8, nodes)), blocks, goal,
+        body_force, shift_coef, jnp.broadcast_to(ids[None], (8, nodes)), ids[:, None], place, blocks, gap,
     )
 
-    flat = jnp.zeros((COMP * cell_total,), jnp.float32).at[dof_index.reshape(-1)].add(force[:COMP].reshape(-1))
-    velocity = smooth(body_force - flat.reshape(body_force.shape), shift_coef)
     back = lax.all_to_all(multi[:MULT, :slots], "gx", split_axis=1, concat_axis=1, tiled=True)
     multipliers = jnp.dot(back, choose.T, precision=lax.Precision.HIGHEST)
     return (multipliers, velocity)

time: 172 us -> 123 us (0.72); the launches traced: 170 us -> 123 us
  local copies, waits for them, and re-layouts: 42.7 us -> 12.8 us
  other arithmetic: 29 us -> 4 us
  starting transfers between devices: 24.9 us -> 3.34 us
  blocking collectives: 0 us -> 20 us
  Pallas kernels: 61.9 us -> 75.7 us
  waiting for transfers between devices: 8.68 us -> 4.69 us
    gather x2 -> x0, local copies, waits for them, and re-layouts: 23.6 us -> none  [the longest x1 17.4 us: shards(): smooth(body_force, shift_coef).reshape(-1)[dof_index]]
    all_to_all x0 -> x1, blocking collectives: none -> 20 us  [shards(): moved = lax.all_to_all(held, 'gx', split_axis=1, concat_axis=1, tiled=True)]
    scatter-add x1 -> x0, other arithmetic: 17.8 us -> none  [shards(): jnp.zeros((COMP * cell_total,), jnp.float32).at[dof_index.reshape(-1)]]
    ppermute x8 -> x0, starting transfers between devices: 16.3 us -> none  [the longest x4 11.1 us: halo(): before = lax.ppermute(tail, axis, [(i, i + 1) for i in range(count - 1)])]
    pallas_call x1, Pallas kernels: 61.9 us -> 75.7 us  [shards(): pl.pallas_call(functools.partial(uzawa_kernel, groups, rows_gy, slots, (f...]
    ppermute x8 -> x0, waiting for transfers between devices: 8.52 us -> none  [the longest x4 8.11 us: halo(): after = lax.ppermute(head, axis, [(i + 1, i) for i in range(count - 1)])]
    all_to_all x1 -> x0, starting transfers between devices: 5.3 us -> none  [shards(): moved = lax.all_to_all(held, 'gx', split_axis=1, concat_axis=1, tiled=True)]
    all_to_all x1, waiting for transfers between devices: 0.01 us -> 4.69 us  [shards(): lax.all_to_all(multi[:MULT, :slots], 'gx', split_axis=1, concat_axis=1, t...]
  transfers between devices with their start and end apart: 10 -> 1, of which waited for: 4 -> 1; matrix products, arithmetic and copies ran while one was open for 1% -> 0% of each run, Pallas kernels for 0% -> 0%
where the time goes in v2:
time: 123 us
  Pallas kernels  75.7 us (62%)
  blocking collectives  20 us (16%)
  local copies, waits for them, and re-layouts  12.8 us (10%)
  waiting for transfers between devices  4.69 us (4%)
  other arithmetic  4 us (3%)
  starting transfers between devices  3.34 us (3%)
  matrix products  1.48 us (1%)
    pallas_call x1, Pallas kernels, shards(): pl.pallas_call(functools.partial(uzawa_kernel, groups, rows_gy, slots, (f...  75.7 us
    all_to_all x1, blocking collectives, shards(): moved = lax.all_to_all(held, 'gx', split_axis=1, concat_axis=1, tiled=True)  20 us
    all_to_all x1, waiting for transfers between devices, shards(): lax.all_to_all(multi[:MULT, :slots], 'gx', split_axis=1, concat_axis=1, t...  4.69 us
    all_to_all x1, starting transfers between devices, shards(): lax.all_to_all(multi[:MULT, :slots], 'gx', split_axis=1, concat_axis=1, t...  3.34 us
    reshape x1, local copies, waits for them, and re-layouts, shards(): blocks = moved[:block_rows].reshape(COMP * quads, pack, MULT, slots)  3.07 us
    unnamed x5, local copies, waits for them, and re-layouts  2.56 us
  transfers between devices with their start and end apart: 1, of which 1 were waited for; matrix products, arithmetic and copies ran while one was open for 0% of the time, Pallas kernels for 0%

profile of v2, /device:TPU:0, one launch (start us, length us, event | category | flops | bytes accessed | tf_op | source)
XLA Modules:
  0.0 122.8 jit_solution(14709250398892886092)
XLA Ops:
  0.6 0.7 convert_element_type.91
  1.4 0.1 copy.53
  1.4 0.7 fusion.12
  2.2 0.1 reduce_window_sum.11
  2.2 0.8 select_reduce_fusion
  3.0 0.7 fusion.24
  3.7 1.3 %concatenate.3 = f32[7889,32]{0,1:T(8,128)S(1)} concatenate(f32[7776,32]{0,1:T(8,128)} %param.8, f32[32,32]{0,1:T(8,128)S(1)} %copy.53, f32[81,32]{0,1:T(8,128)} %param.10), dimensions={0} | concatenate | bytes 2019584 | tf_op jit(solution)/shard_map/concatenate | solution.py:250
  5.0 0.7 fusion.11
  5.7 0.3 all_to_all.14
  6.0 20.0 %all_to_all.21 = f32[7889,8,4]{0,2,1:T(4,128)S(1)} all-to-all(f32[7889,8,4]{0,2,1:T(4,128)S(1)} %all_to_all.14), channel_id=1, replica_groups=mesh['gx'=8,'gy'=4] {'gx'}, dimensions={1} | all-to-all | bytes 2019584 | tf_op jit(solution)/shard_map/all_to_all | solution.py:253
  26.0 0.1 slice.22
  26.0 0.1 copy.55
  26.2 0.1 convert_element_type.98
  26.3 0.1 convert_element_type.94
  26.4 0.2 convert_element_type.99
  26.7 0.1 copy.65.gap_ref
  26.9 0.9 fusion.4.col_ref
  27.8 0.1 slice.23
  27.9 3.1 %reshape.340 = f32[24,4,81,32]{2,1,0,3:T(4,128)S(1)} reshape(f32[7776,8,4]{0,2,1:T(4,128)S(1)} %slice.23) | data formatting | bytes 1990656 | tf_op jit(solution)/shard_map/reshape | solution.py:255
  30.9 2.1 %copy.63 = f32[24,81,4,32]{1,3,2,0:T(8,128)} copy(f32[24,81,4,32]{1,2,0,3:T(4,128)S(1)} %bitcast.21) | data formatting | bytes 1990656 | tf_op jit(solution)/shard_map/transpose | solution.py:256
  33.0 1.9 %copy.64 = f32[24,81,128]{2,1,0:T(8,128)S(1)} copy(f32[24,81,128]{1,2,0:T(8,128)} %bitcast.22) | data formatting | bytes 1990656 | tf_op jit(solution)/shard_map/reshape | solution.py:256
  34.9 0.0 copy-start
  34.9 0.0 copy-start.1
  34.9 0.1 pad.13.block_ref
  35.0 1.3 %copy-done = f32[3,32,32,128]{3,2,1,0:T(8,128)S(1)} copy-done((f32[3,32,32,128]{3,2,1,0:T(8,128)S(1)}, f32[3,32,32,128]{3,2,1,0:T(8,128)}, u32[]{:S(2)}) %copy-start) | copy-done | bytes 1572888
  36.3 0.1 copy-done.1
  36.4 75.7 %shard_map.77 = (f32[88,128]{1,0:T(8,128)S(1)}, f32[3,32,32,128]{3,2,1,0:T(8,128)S(1)}) custom-call(f32[3,32,32,128]{3,2,1,0:T(8,128)S(1)} %copy-done, f32[32,32,128]{2,1,0:T(8,128)S(1)} %copy-done.1, f32[8,1024]{1,0:T(8,128)S(1)} %broadcast_in_dim.2.row_ref, f32[1024,1]{1,0:T(8,128)S(1)} %fusion.4.col_ref, s32[8,1024]{1,0:T(8,128)S(1)} %pad.12.place_ref, ...), custom_call_target="tpu_custom_call" | custom-call | tf_op jit(solution)/shard_map/pallas_call | solution.py:267
  112.1 0.7 copy.66
  112.8 3.3 %all-to-all-start.1 = ((f32[81,8,4]{0,2,1:T(4,128)}), f32[81,8,4]{0,2,1:T(4,128)S(1)}, u32[]{:S(2)}, u32[]{:S(2)}) async-start(f32[81,8,4]{0,2,1:T(4,128)} %bitcast.7), calls=%async_computation.1 | async-start | bytes 32768 | tf_op jit(solution)/shard_map/all_to_all | solution.py:301
  116.2 4.7 %all-to-all-done.1 = f32[81,8,4]{0,2,1:T(4,128)S(1)} async-done(((f32[81,8,4]{0,2,1:T(4,128)}), f32[81,8,4]{0,2,1:T(4,128)S(1)}, u32[]{:S(2)}, u32[]{:S(2)}) %all-to-all-start.1) | async-done | bytes 10400 | tf_op jit(solution)/shard_map/all_to_all | solution.py:301
  120.8 0.8 fusion.10
  121.6 1.1 copy.72
  (10 shorter events, 0.1 us)
Async XLA Ops:
  34.9 1.4 %copy-start = (f32[3,32,32,128]{3,2,1,0:T(8,128)S(1)}, f32[3,32,32,128]{3,2,1,0:T(8,128)}, u32[]{:S(2)}) copy-start(f32[3,32,32,128]{3,2,1,0:T(8,128)} %force_ref.1) | copy-start | bytes 4718596
  34.9 1.5 %copy-start.1 = (f32[32,32,128]{2,1,0:T(8,128)S(1)}, f32[32,32,128]{2,1,0:T(8,128)}, u32[]{:S(2)}) copy-start(f32[32,32,128]{2,1,0:T(8,128)} %shift_ref.1) | copy-start | bytes 1572868
  112.8 8.0 %all-to-all-start.1 = ((f32[81,8,4]{0,2,1:T(4,128)}), f32[81,8,4]{0,2,1:T(4,128)S(1)}, u32[]{:S(2)}, u32[]{:S(2)}) async-start(f32[81,8,4]{0,2,1:T(4,128)} %bitcast.7), calls=%async_computation.1 | async-start | bytes 32768 | tf_op jit(solution)/shard_map/all_to_all | solution.py:301

commit v3 on v2

--- a/solution.py
+++ b/solution.py
@@ -180,51 +180,81 @@
             shift //= 2
         return image
 
-    def all_sum(slot):
-        for axis, me, count, source, room, sems in (
-            ("gx", me_x, ngx, part, line, line_sem), ("gy", me_y, ngy, total, far, far_sem)):
-            copies = []
-            for o in range(1, count):
-                copy = pltpu.make_async_remote_copy(
-                    src_ref=source, dst_ref=room.at[slot, o],
-                    send_sem=sems.at[0, slot, o], recv_sem=sems.at[1, slot, o],
-                    device_id={axis: lax.rem(me + o, count)}, device_id_type=MESH)
-                copy.start()
-                copies.append(copy)
-            summed = source[...]
-            for o, copy in enumerate(copies):
-                copy.wait()
-                summed = summed + room[slot, o + 1]
-            if axis == "gx":
-                total[...] = summed
+    def send_part(slot, stage):
+        axis, me, count, source, room, sems = (
+            ("gx", me_x, ngx, part, line, line_sem), ("gy", me_y, ngy, total, far, far_sem))[stage]
+        copies = []
+        for o in range(1, count):
+            copy = pltpu.make_async_remote_copy(
+                src_ref=source, dst_ref=room.at[slot, o],
+                send_sem=sems.at[0, slot, o], recv_sem=sems.at[1, slot, o],
+                device_id={axis: lax.rem(me + o, count)}, device_id_type=MESH)
+            copy.start()
+            copies.append(copy)
+        return copies
+
+    def add_parts(copies, slot, stage):
+        source, room = ((part, line), (total, far))[stage]
+        summed = source[...]
+        for o, copy in enumerate(copies):
+            copy.wait()
+            summed = summed + room[slot, o + 1]
         return summed
 
-    def step(iteration, state):
-        multi, residual, direction = state
-        apply_bt(direction, sent)
+    def start_image(field, slot):
+        apply_bt(field, sent)
         scaled = sent[...] * inverse
         sent[...] = scaled
-        copies = exchange(sent, iteration + 1)
-        here = apply_link(0, scaled)
-        beside = apply_link(1, scaled)
+        return scaled, exchange(sent, slot)
+
+    def local_image(scaled):
+        return apply_link(0, scaled), apply_link(1, scaled)
+
+    def finish_image(copies, slot, here, beside):
         for side, copy in enumerate(copies):
             copy.wait()
-            beside = beside + apply_link(2 + side, got[iteration + 1, side])
-        image = apply_b(here + beside * inverse)
+            beside = beside + apply_link(2 + side, got[slot, side])
+        return apply_b(here + beside * inverse)
+
+    def form_part(residual, direction, image):
         for row, (a, b) in enumerate(
             ((residual, residual), (direction, image), (residual, image), (image, image))):
             part[row:row + 1, :] = jnp.sum(a * b, axis=0, keepdims=True)
-        sums = jnp.sum(all_sum(iteration), axis=1, keepdims=True)
+
+    def coefficients(tile_sum):
+        sums = jnp.sum(tile_sum, axis=1, keepdims=True)
         norm_now, bend, cross, square = sums[0:1], sums[1:2], sums[2:3], sums[3:4]
         step_size = norm_now / bend
         norm_next = norm_now - 2.0 * step_size * cross + step_size * step_size * square
+        return step_size, norm_next / norm_now
+
+    def step(iteration, state):
+        multi, residual, direction, image, reach = state
+        form_part(residual, direction, image)
+        parts = send_part(iteration, 0)
+        scaled, copies = start_image(image, iteration + 2)
+        here, beside = local_image(scaled)
+        total[...] = add_parts(parts, iteration, 0)
+        parts = send_part(iteration, 1)
+        second = finish_image(copies, iteration + 2, here, beside)
+        step_size, ratio = coefficients(add_parts(parts, iteration, 1))
         multi = multi + step_size * direction
         residual = residual - step_size * image
-        direction = residual + norm_next / norm_now * direction
-        return multi, residual, direction
+        reach = reach - step_size * second
+        direction = residual + ratio * direction
+        image = reach + ratio * image
+        return multi, residual, direction, image, reach
 
     goal = apply_b(start) - gap_ref[...]
-    multi, _, _ = lax.fori_loop(0, ITERS, step, (jnp.zeros_like(goal), goal, goal))
+    scaled, copies = start_image(goal, 1)
+    here, beside = local_image(scaled)
+    image = finish_image(copies, 1, here, beside)
+    multi, residual, direction, image, _ = lax.fori_loop(
+        0, ITERS - 1, step, (jnp.zeros_like(goal), goal, goal, image, image))
+    form_part(residual, direction, image)
+    total[...] = add_parts(send_part(ITERS - 1, 0), ITERS - 1, 0)
+    step_size, _ = coefficients(add_parts(send_part(ITERS - 1, 1), ITERS - 1, 1))
+    multi = multi + step_size * direction
     mult_ref[...] = multi
     apply_bt(multi, sent)
     if spot < 6:

time: 123 us -> 106 us (0.86)
  Pallas kernels: 75.7 us -> 58.8 us
    pallas_call x1, Pallas kernels: 75.7 us -> 58.8 us  [shards(): pl.pallas_call(functools.partial(uzawa_kernel, groups, rows_gy, slots, (f...]
where the time goes in v3:
time: 106 us
  Pallas kernels  58.8 us (55%)
  blocking collectives  20 us (19%)
  local copies, waits for them, and re-layouts  12.8 us (12%)
  waiting for transfers between devices  4.69 us (4%)
  other arithmetic  4 us (4%)
  starting transfers between devices  3.34 us (3%)
  matrix products  1.48 us (1%)
    pallas_call x1, Pallas kernels, shards(): pl.pallas_call(functools.partial(uzawa_kernel, groups, rows_gy, slots, (f...  58.8 us
    all_to_all x1, blocking collectives, shards(): moved = lax.all_to_all(held, 'gx', split_axis=1, concat_axis=1, tiled=True)  20 us
    all_to_all x1, waiting for transfers between devices, shards(): lax.all_to_all(multi[:MULT, :slots], 'gx', split_axis=1, concat_axis=1, t...  4.69 us
    all_to_all x1, starting transfers between devices, shards(): lax.all_to_all(multi[:MULT, :slots], 'gx', split_axis=1, concat_axis=1, t...  3.34 us
    reshape x1, local copies, waits for them, and re-layouts, shards(): blocks = moved[:block_rows].reshape(COMP * quads, pack, MULT, slots)  3.07 us
    unnamed x5, local copies, waits for them, and re-layouts  2.56 us
  transfers between devices with their start and end apart: 1, of which 1 were waited for; matrix products, arithmetic and copies ran while one was open for 0% of the time, Pallas kernels for 0%

profile of v3, /device:TPU:0, one launch (start us, length us, event | category | flops | bytes accessed | tf_op | source)
XLA Modules:
  0.0 105.9 jit_solution(3035967545377236533)
XLA Ops:
  0.6 0.7 convert_element_type.91
  1.4 0.1 copy.53
  1.4 0.7 fusion.12
  2.2 0.1 reduce_window_sum.11
  2.2 0.8 select_reduce_fusion
  3.0 0.7 fusion.24
  3.7 1.3 %concatenate.3 = f32[7889,32]{0,1:T(8,128)S(1)} concatenate(f32[7776,32]{0,1:T(8,128)} %param.8, f32[32,32]{0,1:T(8,128)S(1)} %copy.53, f32[81,32]{0,1:T(8,128)} %param.10), dimensions={0} | concatenate | bytes 2019584 | tf_op jit(solution)/shard_map/concatenate | solution.py:280
  5.0 0.7 fusion.11
  5.7 0.3 all_to_all.14
  6.0 20.0 %all_to_all.21 = f32[7889,8,4]{0,2,1:T(4,128)S(1)} all-to-all(f32[7889,8,4]{0,2,1:T(4,128)S(1)} %all_to_all.14), channel_id=1, replica_groups=mesh['gx'=8,'gy'=4] {'gx'}, dimensions={1} | all-to-all | bytes 2019584 | tf_op jit(solution)/shard_map/all_to_all | solution.py:283
  26.0 0.1 slice.22
  26.0 0.1 copy.55
  26.2 0.1 convert_element_type.98
  26.3 0.1 convert_element_type.94
  26.4 0.2 convert_element_type.99
  26.7 0.1 copy.65.gap_ref
  26.9 0.9 fusion.4.col_ref
  27.8 0.1 slice.23
  27.9 3.1 %reshape.340 = f32[24,4,81,32]{2,1,0,3:T(4,128)S(1)} reshape(f32[7776,8,4]{0,2,1:T(4,128)S(1)} %slice.23) | data formatting | bytes 1990656 | tf_op jit(solution)/shard_map/reshape | solution.py:285
  30.9 2.1 %copy.63 = f32[24,81,4,32]{1,3,2,0:T(8,128)} copy(f32[24,81,4,32]{1,2,0,3:T(4,128)S(1)} %bitcast.21) | data formatting | bytes 1990656 | tf_op jit(solution)/shard_map/transpose | solution.py:286
  33.0 1.9 %copy.64 = f32[24,81,128]{2,1,0:T(8,128)S(1)} copy(f32[24,81,128]{1,2,0:T(8,128)} %bitcast.22) | data formatting | bytes 1990656 | tf_op jit(solution)/shard_map/reshape | solution.py:286
  34.9 0.0 copy-start
  34.9 0.0 copy-start.1
  34.9 0.1 pad.13.block_ref
  35.0 1.3 %copy-done = f32[3,32,32,128]{3,2,1,0:T(8,128)S(1)} copy-done((f32[3,32,32,128]{3,2,1,0:T(8,128)S(1)}, f32[3,32,32,128]{3,2,1,0:T(8,128)}, u32[]{:S(2)}) %copy-start) | copy-done | bytes 1572888
  36.3 0.1 copy-done.1
  36.4 58.8 %shard_map.77 = (f32[88,128]{1,0:T(8,128)S(1)}, f32[3,32,32,128]{3,2,1,0:T(8,128)S(1)}) custom-call(f32[3,32,32,128]{3,2,1,0:T(8,128)S(1)} %copy-done, f32[32,32,128]{2,1,0:T(8,128)S(1)} %copy-done.1, f32[8,1024]{1,0:T(8,128)S(1)} %broadcast_in_dim.2.row_ref, f32[1024,1]{1,0:T(8,128)S(1)} %fusion.4.col_ref, s32[8,1024]{1,0:T(8,128)S(1)} %pad.12.place_ref, ...), custom_call_target="tpu_custom_call" | custom-call | tf_op jit(solution)/shard_map/pallas_call | solution.py:297
  95.3 0.7 copy.66
  96.0 3.3 %all-to-all-start.1 = ((f32[81,8,4]{0,2,1:T(4,128)}), f32[81,8,4]{0,2,1:T(4,128)S(1)}, u32[]{:S(2)}, u32[]{:S(2)}) async-start(f32[81,8,4]{0,2,1:T(4,128)} %bitcast.7), calls=%async_computation.1 | async-start | bytes 32768 | tf_op jit(solution)/shard_map/all_to_all | solution.py:331
  99.3 4.7 %all-to-all-done.1 = f32[81,8,4]{0,2,1:T(4,128)S(1)} async-done(((f32[81,8,4]{0,2,1:T(4,128)}), f32[81,8,4]{0,2,1:T(4,128)S(1)}, u32[]{:S(2)}, u32[]{:S(2)}) %all-to-all-start.1) | async-done | bytes 10400 | tf_op jit(solution)/shard_map/all_to_all | solution.py:331
  104.0 0.8 fusion.10
  104.8 1.1 %copy.72 = f32[3,32,32,128]{3,2,1,0:T(8,128)} copy(f32[3,32,32,128]{3,2,1,0:T(8,128)S(1)} %get-tuple-element.11) | data formatting | bytes 3145728
  (10 shorter events, 0.1 us)
Async XLA Ops:
  34.9 1.4 %copy-start = (f32[3,32,32,128]{3,2,1,0:T(8,128)S(1)}, f32[3,32,32,128]{3,2,1,0:T(8,128)}, u32[]{:S(2)}) copy-start(f32[3,32,32,128]{3,2,1,0:T(8,128)} %force_ref.1) | copy-start | bytes 4718596
  34.9 1.5 %copy-start.1 = (f32[32,32,128]{2,1,0:T(8,128)S(1)}, f32[32,32,128]{2,1,0:T(8,128)}, u32[]{:S(2)}) copy-start(f32[32,32,128]{2,1,0:T(8,128)} %shift_ref.1) | copy-start | bytes 1572868
  96.0 8.0 %all-to-all-start.1 = ((f32[81,8,4]{0,2,1:T(4,128)}), f32[81,8,4]{0,2,1:T(4,128)S(1)}, u32[]{:S(2)}, u32[]{:S(2)}) async-start(f32[81,8,4]{0,2,1:T(4,128)} %bitcast.7), calls=%async_computation.1 | async-start | bytes 32768 | tf_op jit(solution)/shard_map/all_to_all | solution.py:331

commit v4 on v3

--- a/solution.py
+++ b/solution.py
@@ -22,7 +22,7 @@
 
 def uzawa_kernel(ngx, ngy, slots, strides, spans, force_ref, shift_ref, row_ref, col_ref,
                  place_ref, block_ref, gap_ref, mult_ref, out_ref, links, inv, grown, edge, face, sent, got, part,
-                 line, total, far, face_sem, swap_sem, line_sem, far_sem):
+                 line, total, far, own, home, face_sem, home_sem, swap_sem, line_sem, far_sem):
     me_x, me_y = lax.axis_index("gx"), lax.axis_index("gy")
     nodes = row_ref.shape[1]
     quads = nodes // 128
@@ -255,13 +255,29 @@
     total[...] = add_parts(send_part(ITERS - 1, 0), ITERS - 1, 0)
     step_size, _ = coefficients(add_parts(send_part(ITERS - 1, 1), ITERS - 1, 1))
     multi = multi + step_size * direction
-    mult_ref[...] = multi
+    own[...] = multi
+    returns = []
+    for o in range(1, ngx):
+        copy = pltpu.make_async_remote_copy(
+            src_ref=own, dst_ref=home.at[o], send_sem=home_sem.at[0, o], recv_sem=home_sem.at[1, o],
+            device_id={"gx": lax.rem(me_x + o, ngx)}, device_id_type=MESH)
+        copy.start()
+        returns.append(copy)
     apply_bt(multi, sent)
     if spot < 6:
         mark_spots()
     for c in range(COMP):
         grown[c, 1:cx + 1] = (force_ref[c] - scatter(sent[c:c + 1, :])) * inv[...]
     finish_smooth(start_faces(1), 1)
+    lane = lax.broadcasted_iota(jnp.int32, (ROWS, 128), 1) // CAP
+    collected = jnp.zeros((ROWS, 128), jnp.float32)
+    for o in range(ngx):
+        if o:
+            returns[o - 1].wait()
+        tile_of = home[o] if o else own[...]
+        turned = pltpu.roll(tile_of, lax.rem(o * CAP + 128 - me_x * CAP, 128), 1)
+        collected = jnp.where(lane == o, turned, collected)
+    mult_ref[...] = collected
 
 
 def shards(body_force, shift_coef, coupling, node_cells, target_gap, new_owner):
@@ -316,7 +332,10 @@
             pltpu.VMEM((ITERS, groups, 8, 128), jnp.float32),
             pltpu.VMEM((8, 128), jnp.float32),
             pltpu.VMEM((ITERS, rows_gy, 8, 128), jnp.float32),
+            pltpu.VMEM((ROWS, 128), jnp.float32),
+            pltpu.VMEM((groups, ROWS, 128), jnp.float32),
             pltpu.SemaphoreType.DMA((2, 2, 4)),
+            pltpu.SemaphoreType.DMA((2, groups)),
             pltpu.SemaphoreType.DMA((2, ITERS + 1, 4)),
             pltpu.SemaphoreType.DMA((2, ITERS, groups)),
             pltpu.SemaphoreType.DMA((2, ITERS, rows_gy)),
@@ -328,8 +347,9 @@
         body_force, shift_coef, jnp.broadcast_to(ids[None], (8, nodes)), ids[:, None], place, blocks, gap,
     )
 
-    back = lax.all_to_all(multi[:MULT, :slots], "gx", split_axis=1, concat_axis=1, tiled=True)
-    multipliers = jnp.dot(back, choose.T, precision=lax.Precision.HIGHEST)
+    column = lax.rem(lax.axis_index("gx") - owners + groups, groups) * CAP + rank_in
+    pick = (jnp.arange(128, dtype=jnp.int32)[:, None] == column[None, :]).astype(jnp.float32)
+    multipliers = jnp.dot(multi[:MULT], pick, precision=lax.Precision.HIGHEST)
     return (multipliers, velocity)
 
 

time: 106 us -> 100 us (0.943)
  blocking collectives: 20 us -> 0 us
  waiting for transfers between devices: 4.69 us -> 15 us
  starting transfers between devices: 3.34 us -> 5.17 us
    all_to_all x1 -> x0, blocking collectives: 20 us -> none  [shards(): moved = lax.all_to_all(held, 'gx', split_axis=1, concat_axis=1, tiled=True)]
    all_to_all x1, waiting for transfers between devices: 4.69 us -> 15 us  [shards(): moved = lax.all_to_all(held, 'gx', split_axis=1, concat_axis=1, tiled=True)]
    all_to_all x1, starting transfers between devices: 3.34 us -> 5.17 us  [shards(): moved = lax.all_to_all(held, 'gx', split_axis=1, concat_axis=1, tiled=True)]
    unnamed x5 -> x7, local copies, waits for them, and re-layouts: 2.56 us -> 2.56 us
where the time goes in v4:
time: 100 us; the launch traced here: 99.2 us
  Pallas kernels  59.6 us (60%)
  waiting for transfers between devices  15 us (15%)
  local copies, waits for them, and re-layouts  13.1 us (13%)
  starting transfers between devices  5.17 us (5%)
  other arithmetic  4.01 us (4%)
  matrix products  1.51 us (2%)
    pallas_call x1, Pallas kernels, shards(): pl.pallas_call(functools.partial(uzawa_kernel, groups, rows_gy, slots, (f...  59.6 us
    all_to_all x1, waiting for transfers between devices, shards(): moved = lax.all_to_all(held, 'gx', split_axis=1, concat_axis=1, tiled=True)  15 us
    all_to_all x1, starting transfers between devices, shards(): moved = lax.all_to_all(held, 'gx', split_axis=1, concat_axis=1, tiled=True)  5.17 us
    reshape x1, local copies, waits for them, and re-layouts, shards(): blocks = moved[:block_rows].reshape(COMP * quads, pack, MULT, slots)  3.07 us
    unnamed x7, local copies, waits for them, and re-layouts  2.56 us
    transpose x1, local copies, waits for them, and re-layouts, shards(): blocks.transpose(0, 2, 1, 3).reshape(COMP * quads, MULT, 128)  2.06 us
  transfers between devices with their start and end apart: 1, of which 1 were waited for; matrix products, arithmetic and copies ran while one was open for 0% of the time, Pallas kernels for 0%

profile of v4, /device:TPU:0, one launch (start us, length us, event | category | flops | bytes accessed | tf_op | source)
XLA Modules:
  0.0 99.2 jit_solution(7557519726588736978)
XLA Ops:
  0.6 0.7 convert_element_type.92
  1.4 0.1 copy.50
  1.4 0.7 fusion.13
  2.2 0.1 reduce_window_sum.11
  2.2 0.8 select_reduce_fusion
  3.0 0.7 fusion.28
  3.7 1.3 %concatenate.3 = f32[7889,32]{0,1:T(8,128)S(1)} concatenate(f32[7776,32]{0,1:T(8,128)} %param.8, f32[32,32]{0,1:T(8,128)S(1)} %copy.50, f32[81,32]{0,1:T(8,128)} %param.10), dimensions={0} | concatenate | bytes 2019584 | tf_op jit(solution)/shard_map/concatenate | solution.py:296
  5.0 0.7 fusion.14
  5.7 0.0 copy-start.2
  5.7 1.2 %all_to_all.6 = f32[7889,8,4]{0,2,1:T(4,128)} reshape(f32[7889,32]{0,1:T(8,128)S(1)} %fusion.14) | data formatting | bytes 2019584 | tf_op jit(solution)/shard_map/all_to_all | solution.py:299
  6.9 5.2 %all-to-all-start = ((f32[7889,8,4]{0,2,1:T(4,128)}), f32[7889,8,4]{0,2,1:T(4,128)S(1)}, u32[]{:S(2)}, u32[]{:S(2)}) async-start(f32[7889,8,4]{0,2,1:T(4,128)} %all_to_all.6), calls=%async_computation | async-start | bytes 2031616 | tf_op jit(solution)/shard_map/all_to_all | solution.py:299
  12.1 0.0 copy-done.2
  12.1 15.0 %all-to-all-done = f32[7889,8,4]{0,2,1:T(4,128)S(1)} async-done(((f32[7889,8,4]{0,2,1:T(4,128)}), f32[7889,8,4]{0,2,1:T(4,128)S(1)}, u32[]{:S(2)}, u32[]{:S(2)}) %all-to-all-start) | async-done | bytes 1009824 | tf_op jit(solution)/shard_map/all_to_all | solution.py:299
  27.2 0.1 slice.22
  27.3 0.1 copy.52
  27.4 0.1 convert_element_type.99
  27.5 0.1 convert_element_type.95
  27.7 0.2 convert_element_type.100
  27.9 0.1 copy.62.gap_ref
  28.1 0.9 fusion.4.col_ref
  29.0 0.1 slice.23
  29.1 3.1 %reshape.354 = f32[24,4,81,32]{2,1,0,3:T(4,128)S(1)} reshape(f32[7776,8,4]{0,2,1:T(4,128)S(1)} %slice.23) | data formatting | bytes 1990656 | tf_op jit(solution)/shard_map/reshape | solution.py:301
  32.1 2.1 %copy.60 = f32[24,81,4,32]{1,3,2,0:T(8,128)} copy(f32[24,81,4,32]{1,2,0,3:T(4,128)S(1)} %bitcast.17) | data formatting | bytes 1990656 | tf_op jit(solution)/shard_map/transpose | solution.py:302
  34.2 1.9 %copy.61 = f32[24,81,128]{2,1,0:T(8,128)S(1)} copy(f32[24,81,128]{1,2,0:T(8,128)} %bitcast.18) | data formatting | bytes 1990656 | tf_op jit(solution)/shard_map/reshape | solution.py:302
  36.1 0.0 copy-start
  36.1 0.0 copy-start.1
  36.2 0.1 pad.13.block_ref
  36.2 1.3 %copy-done = f32[3,32,32,128]{3,2,1,0:T(8,128)S(1)} copy-done((f32[3,32,32,128]{3,2,1,0:T(8,128)S(1)}, f32[3,32,32,128]{3,2,1,0:T(8,128)}, u32[]{:S(2)}) %copy-start) | copy-done | bytes 1572888
  37.6 0.1 copy-done.1
  37.7 59.6 %shard_map.77 = (f32[88,128]{1,0:T(8,128)S(1)}, f32[3,32,32,128]{3,2,1,0:T(8,128)S(1)}) custom-call(f32[3,32,32,128]{3,2,1,0:T(8,128)S(1)} %copy-done, f32[32,32,128]{2,1,0:T(8,128)S(1)} %copy-done.1, f32[8,1024]{1,0:T(8,128)S(1)} %broadcast_in_dim.2.row_ref, f32[1024,1]{1,0:T(8,128)S(1)} %fusion.4.col_ref, s32[8,1024]{1,0:T(8,128)S(1)} %pad.12.place_ref, ...), custom_call_target="tpu_custom_call" | custom-call | tf_op jit(solution)/shard_map/pallas_call | solution.py:313
  97.3 0.8 fusion.9
  98.1 1.1 %copy.68 = f32[3,32,32,128]{3,2,1,0:T(8,128)} copy(f32[3,32,32,128]{3,2,1,0:T(8,128)S(1)} %get-tuple-element.11) | data formatting | bytes 3145728
  (11 shorter events, 0.1 us)
Async XLA Ops:
  5.7 6.4 %copy-start.2 = (s32[32,1]{0,1:T(1,128)S(1)}, s32[32,1]{0,1:T(1,128)}, u32[]{:S(2)}) copy-start(s32[32,1]{0,1:T(1,128)} %param.11) | copy-start | bytes 388
  6.9 20.2 %all-to-all-start = ((f32[7889,8,4]{0,2,1:T(4,128)}), f32[7889,8,4]{0,2,1:T(4,128)S(1)}, u32[]{:S(2)}, u32[]{:S(2)}) async-start(f32[7889,8,4]{0,2,1:T(4,128)} %all_to_all.6), calls=%async_computation | async-start | bytes 2031616 | tf_op jit(solution)/shard_map/all_to_all | solution.py:299
  36.1 1.4 %copy-start = (f32[3,32,32,128]{3,2,1,0:T(8,128)S(1)}, f32[3,32,32,128]{3,2,1,0:T(8,128)}, u32[]{:S(2)}) copy-start(f32[3,32,32,128]{3,2,1,0:T(8,128)} %force_ref.1) | copy-start | bytes 4718596
  36.1 1.5 %copy-start.1 = (f32[32,32,128]{2,1,0:T(8,128)S(1)}, f32[32,32,128]{2,1,0:T(8,128)}, u32[]{:S(2)}) copy-start(f32[32,32,128]{2,1,0:T(8,128)} %shift_ref.1) | copy-start | bytes 1572868

commit v5 on v4

--- a/solution.py
+++ b/solution.py
@@ -280,6 +280,25 @@
     mult_ref[...] = collected
 
 
+def move_kernel(count, from_ref, to_ref, send_sem, recv_sem):
+    me = lax.axis_index("gx")
+    barrier = pltpu.get_barrier_semaphore()
+    for o in range(1, count):
+        pl.semaphore_signal(barrier, inc=1, device_id={"gx": lax.rem(me + o, count)}, device_id_type=MESH)
+    pl.semaphore_wait(barrier, count - 1)
+    copies = []
+    for o in range(1, count):
+        peer = lax.rem(me + o, count)
+        copy = pltpu.make_async_remote_copy(
+            src_ref=from_ref.at[peer], dst_ref=to_ref.at[me], send_sem=send_sem.at[o], recv_sem=recv_sem.at[o],
+            device_id={"gx": peer}, device_id_type=MESH)
+        copy.start()
+        copies.append(copy)
+    to_ref[me] = from_ref[me]
+    for copy in copies:
+        copy.wait()
+
+
 def shards(body_force, shift_coef, coupling, node_cells, target_gap, new_owner):
     groups, rows_gy = lax.axis_size("gx"), lax.axis_size("gy")
     slots = groups * CAP
@@ -296,7 +315,17 @@
     held = jnp.concatenate([coupling, node_cells.astype(jnp.float32), target_gap], axis=0)
     choose = (slot_of[:, None] == jnp.arange(slots, dtype=jnp.int32)[None, :]).astype(jnp.float32)
     held = jnp.dot(held, choose, precision=lax.Precision.HIGHEST)
-    moved = lax.all_to_all(held, "gx", split_axis=1, concat_axis=1, tiled=True)
+    parted = held.T.reshape(groups, CAP, held.shape[0])
+    moved = pl.pallas_call(
+        functools.partial(move_kernel, groups),
+        out_shape=jax.ShapeDtypeStruct(parted.shape, jnp.float32),
+        in_specs=[pl.BlockSpec(memory_space=pltpu.VMEM)],
+        out_specs=pl.BlockSpec(memory_space=pltpu.VMEM),
+        scratch_shapes=[pltpu.SemaphoreType.DMA((groups,)), pltpu.SemaphoreType.DMA((groups,))],
+        compiler_params=pltpu.CompilerParams(
+            collective_id=1, has_side_effects=True, vmem_limit_bytes=24 << 20),
+    )(parted)
+    moved = moved.reshape(slots, held.shape[0]).T
     block_rows = COMP * NODES * MULT
     blocks = moved[:block_rows].reshape(COMP * quads, pack, MULT, slots)
     blocks = jnp.pad(blocks.transpose(0, 2, 1, 3).reshape(COMP * quads, MULT, 128), ((0, 0), (0, ROWS - MULT), (0, 0)))

time: 100 us -> 96.9 us (0.969)
  Pallas kernels: 59.6 us -> 77 us
  waiting for transfers between devices: 15 us -> 0 us
  starting transfers between devices: 5.17 us -> 0 us
    pallas_call x0 -> x1, Pallas kernels: none -> 15.5 us  [shards(): pl.pallas_call(functools.partial(move_kernel, groups), out_shape=jax.Shap...]
    all_to_all x1 -> x0, waiting for transfers between devices: 15 us -> none  [shards(): moved = lax.all_to_all(held, 'gx', split_axis=1, concat_axis=1, tiled=True)]
    all_to_all x1 -> x0, starting transfers between devices: 5.17 us -> none  [shards(): moved = lax.all_to_all(held, 'gx', split_axis=1, concat_axis=1, tiled=True)]
    pallas_call x1, Pallas kernels: 59.6 us -> 61.5 us  [shards(): pl.pallas_call(functools.partial(uzawa_kernel, groups, rows_gy, slots, (f...]
    reshape x0 -> x5, local copies, waits for them, and re-layouts: none -> 1.33 us  [the longest x3 0.69 us: shards(): jnp.round(moved[block_rows:block_rows + NODES]).astype(jnp.int32)]
    all_to_all x1 -> x0, local copies, waits for them, and re-layouts: 1.25 us -> none  [shards(): moved = lax.all_to_all(held, 'gx', split_axis=1, concat_axis=1, tiled=True)]
    unnamed x7 -> x5, local copies, waits for them, and re-layouts: 2.56 us -> 2.57 us
  transfers between devices with their start and end apart: 1 -> 0, of which waited for: 1 -> 0; matrix products, arithmetic and copies ran while one was open for 0% -> 0% of each run, Pallas kernels for 0% -> 0%
where the time goes in v5:
time: 96.9 us; the launch traced here: 96.6 us
  Pallas kernels  77 us (79%)
  local copies, waits for them, and re-layouts  12.5 us (13%)
  other arithmetic  4.73 us (5%)
  matrix products  1.51 us (2%)
    pallas_call x1, Pallas kernels, shards(): pl.pallas_call(functools.partial(uzawa_kernel, groups, rows_gy, slots, (f...  61.5 us
    pallas_call x1, Pallas kernels, shards(): pl.pallas_call(functools.partial(move_kernel, groups), out_shape=jax.Shap...  15.5 us
    reshape x1, local copies, waits for them, and re-layouts, shards(): blocks = moved[:block_rows].reshape(COMP * quads, pack, MULT, slots)  2.95 us
    unnamed x5, local copies, waits for them, and re-layouts  2.57 us
    transpose x1, local copies, waits for them, and re-layouts, shards(): blocks.transpose(0, 2, 1, 3).reshape(COMP * quads, MULT, 128)  2.06 us

profile of v5, /device:TPU:0, one launch (start us, length us, event | category | flops | bytes accessed | tf_op | source)
XLA Modules:
  0.0 96.6 jit_solution(18181033958468693325)
XLA Ops:
  0.6 0.7 convert_element_type.32
  1.4 0.1 copy.31
  1.4 0.7 fusion.13
  2.2 0.1 reduce_window_sum.11
  2.2 0.8 select_reduce_fusion
  3.0 0.7 fusion.27
  3.7 0.7 fusion.28
  4.4 1.3 %concatenate.3 = f32[7889,32]{0,1:T(8,128)S(1)} concatenate(f32[7776,32]{0,1:T(8,128)} %param.8, f32[32,32]{0,1:T(8,128)S(1)} %copy.31, f32[81,32]{0,1:T(8,128)} %param.10), dimensions={0} | concatenate | bytes 2019584 | tf_op jit(solution)/shard_map/concatenate | solution.py:315
  5.7 0.7 fusion.14
  6.3 0.3 reshape.360.from_ref
  6.7 15.5 %shard_map.77 = f32[8,4,7889]{2,1,0:T(4,128)S(1)} custom-call(f32[8,4,7889]{2,1,0:T(4,128)S(1)} %reshape.360.from_ref), custom_call_target="tpu_custom_call" | custom-call | tf_op jit(solution)/shard_map/pallas_call | solution.py:319
  22.2 0.3 reshape.361
  22.6 0.1 fusion.12
  22.6 0.1 slice.17
  22.7 0.1 copy.32
  22.8 0.1 reshape.364
  22.9 0.1 reshape.362
  23.1 0.1 copy.42.gap_ref
  23.2 0.5 reshape.367
  23.7 0.9 fusion.4.col_ref
  24.6 3.0 %reshape.365 = f32[24,4,81,32]{2,1,0,3:T(4,128)S(1)} reshape(f32[7776,32]{0,1:T(8,128)S(1)} %slice.17) | data formatting | bytes 1990656 | tf_op jit(solution)/shard_map/reshape | solution.py:330
  27.6 2.1 %copy.40 = f32[24,81,4,32]{1,3,2,0:T(8,128)} copy(f32[24,81,4,32]{1,2,0,3:T(4,128)S(1)} %bitcast.15) | data formatting | bytes 1990656 | tf_op jit(solution)/shard_map/transpose | solution.py:331
  29.7 1.9 %copy.41 = f32[24,81,128]{2,1,0:T(8,128)S(1)} copy(f32[24,81,128]{1,2,0:T(8,128)} %bitcast.16) | data formatting | bytes 1990656 | tf_op jit(solution)/shard_map/reshape | solution.py:331
  31.6 0.0 copy-start
  31.6 0.0 copy-start.1
  31.6 0.1 pad.13.block_ref
  31.7 1.3 %copy-done = f32[3,32,32,128]{3,2,1,0:T(8,128)S(1)} copy-done((f32[3,32,32,128]{3,2,1,0:T(8,128)S(1)}, f32[3,32,32,128]{3,2,1,0:T(8,128)}, u32[]{:S(2)}) %copy-start) | copy-done | bytes 1572888
  33.0 0.1 copy-done.1
  33.1 61.5 %shard_map.78 = (f32[88,128]{1,0:T(8,128)S(1)}, f32[3,32,32,128]{3,2,1,0:T(8,128)S(1)}) custom-call(f32[3,32,32,128]{3,2,1,0:T(8,128)S(1)} %copy-done, f32[32,32,128]{2,1,0:T(8,128)S(1)} %copy-done.1, f32[8,1024]{1,0:T(8,128)S(1)} %broadcast_in_dim.2.row_ref, f32[1024,1]{1,0:T(8,128)S(1)} %fusion.4.col_ref, s32[8,1024]{1,0:T(8,128)S(1)} %pad.12.place_ref, ...), custom_call_target="tpu_custom_call" | custom-call | tf_op jit(solution)/shard_map/pallas_call | solution.py:342
  94.6 0.8 fusion.9
  95.4 1.1 %copy.44 = f32[3,32,32,128]{3,2,1,0:T(8,128)} copy(f32[3,32,32,128]{3,2,1,0:T(8,128)S(1)} %get-tuple-element.11) | data formatting | bytes 3145728
  (9 shorter events, 0.1 us)
Async XLA Ops:
  31.6 1.4 %copy-start = (f32[3,32,32,128]{3,2,1,0:T(8,128)S(1)}, f32[3,32,32,128]{3,2,1,0:T(8,128)}, u32[]{:S(2)}) copy-start(f32[3,32,32,128]{3,2,1,0:T(8,128)} %force_ref.1) | copy-start | bytes 4718596
  31.6 1.5 %copy-start.1 = (f32[32,32,128]{2,1,0:T(8,128)S(1)}, f32[32,32,128]{2,1,0:T(8,128)}, u32[]{:S(2)}) copy-start(f32[32,32,128]{2,1,0:T(8,128)} %shift_ref.1) | copy-start | bytes 1572868

commit v6 on v5

--- a/solution.py
+++ b/solution.py
@@ -80,7 +80,7 @@
         y_at = lax.broadcasted_iota(jnp.int32, (cy, cz), 0)
         z_at = lax.broadcasted_iota(jnp.int32, (cy, cz), 1)
 
-        @pl.loop(0, cx)
+        @pl.loop(0, cx, unroll=4)
         def _(x):
             scale = inv[x]
             for c in range(COMP):
@@ -95,7 +95,7 @@
                 out_ref[c, x] = mid + beside * scale
 
     def mark_spots():
-        @pl.loop(0, columns // 128)
+        @pl.loop(0, columns // 128, unroll=2)
         def _(i):
             at = pl.multiple_of(i * 128, 128)
             here = lax.broadcasted_iota(jnp.int32, (128, nodes), 0) + at
@@ -126,7 +126,7 @@
     tile = 128
     mark_spots()
 
-    @pl.loop(0, nodes // tile)
+    @pl.loop(0, nodes // tile, unroll=2)
     def _(i):
         at = pl.ds(pl.multiple_of(i * tile, tile), tile)
         gap = jnp.abs(row_ref[0:1, :] - col_ref[at, :])
@@ -150,7 +150,7 @@
     from_below = jnp.where(me_y > 0, z_step - y_span, nowhere).astype(jnp.float32)
     from_above = jnp.where(me_y < ngy - 1, y_span - z_step, nowhere).astype(jnp.float32)
 
-    @pl.loop(0, nodes // tile)
+    @pl.loop(0, nodes // tile, unroll=2)
     def _(i):
         at = pl.ds(pl.multiple_of(i * tile, tile), tile)
         own = col_ref[at, :]

time: 96.9 us -> 93.1 us (0.961)
  Pallas kernels: 77 us -> 73.2 us
    pallas_call x1, Pallas kernels: 61.5 us -> 57.7 us  [shards(): pl.pallas_call(functools.partial(uzawa_kernel, groups, rows_gy, slots, (f...]
where the time goes in v6:
time: 93.1 us; the launch traced here: 92.8 us
  Pallas kernels  73.2 us (79%)
  local copies, waits for them, and re-layouts  12.5 us (13%)
  other arithmetic  4.73 us (5%)
  matrix products  1.51 us (2%)
    pallas_call x1, Pallas kernels, shards(): pl.pallas_call(functools.partial(uzawa_kernel, groups, rows_gy, slots, (f...  57.7 us
    pallas_call x1, Pallas kernels, shards(): pl.pallas_call(functools.partial(move_kernel, groups), out_shape=jax.Shap...  15.5 us
    reshape x1, local copies, waits for them, and re-layouts, shards(): blocks = moved[:block_rows].reshape(COMP * quads, pack, MULT, slots)  2.95 us
    unnamed x5, local copies, waits for them, and re-layouts  2.57 us
    transpose x1, local copies, waits for them, and re-layouts, shards(): blocks.transpose(0, 2, 1, 3).reshape(COMP * quads, MULT, 128)  2.06 us
    reshape x1, local copies, waits for them, and re-layouts, shards(): blocks.transpose(0, 2, 1, 3).reshape(COMP * quads, MULT, 128)  1.93 us

profile of v6, /device:TPU:0, one launch (start us, length us, event | category | flops | bytes accessed | tf_op | source)
XLA Modules:
  0.0 92.8 jit_solution(12179427908439303215)
XLA Ops:
  0.6 0.7 convert_element_type.32
  1.4 0.1 copy.31
  1.4 0.7 fusion.13
  2.2 0.1 reduce_window_sum.11
  2.2 0.8 select_reduce_fusion
  3.0 0.7 fusion.27
  3.7 0.7 fusion.28
  4.4 1.3 %concatenate.3 = f32[7889,32]{0,1:T(8,128)S(1)} concatenate(f32[7776,32]{0,1:T(8,128)} %param.8, f32[32,32]{0,1:T(8,128)S(1)} %copy.31, f32[81,32]{0,1:T(8,128)} %param.10), dimensions={0} | concatenate | bytes 2019584 | tf_op jit(solution)/shard_map/concatenate | solution.py:315
  5.7 0.7 fusion.14
  6.3 0.3 reshape.360.from_ref
  6.7 15.5 %shard_map.77 = f32[8,4,7889]{2,1,0:T(4,128)S(1)} custom-call(f32[8,4,7889]{2,1,0:T(4,128)S(1)} %reshape.360.from_ref), custom_call_target="tpu_custom_call" | custom-call | tf_op jit(solution)/shard_map/pallas_call | solution.py:319
  22.2 0.3 reshape.361
  22.6 0.1 fusion.12
  22.6 0.1 slice.17
  22.7 0.1 copy.32
  22.8 0.1 reshape.364
  22.9 0.1 reshape.362
  23.1 0.1 copy.42.gap_ref
  23.2 0.5 reshape.367
  23.7 0.9 fusion.4.col_ref
  24.6 3.0 %reshape.365 = f32[24,4,81,32]{2,1,0,3:T(4,128)S(1)} reshape(f32[7776,32]{0,1:T(8,128)S(1)} %slice.17) | data formatting | bytes 1990656 | tf_op jit(solution)/shard_map/reshape | solution.py:330
  27.6 2.1 %copy.40 = f32[24,81,4,32]{1,3,2,0:T(8,128)} copy(f32[24,81,4,32]{1,2,0,3:T(4,128)S(1)} %bitcast.15) | data formatting | bytes 1990656 | tf_op jit(solution)/shard_map/transpose | solution.py:331
  29.7 1.9 %copy.41 = f32[24,81,128]{2,1,0:T(8,128)S(1)} copy(f32[24,81,128]{1,2,0:T(8,128)} %bitcast.16) | data formatting | bytes 1990656 | tf_op jit(solution)/shard_map/reshape | solution.py:331
  31.6 0.0 copy-start
  31.6 0.0 copy-start.1
  31.6 0.1 pad.13.block_ref
  31.7 1.3 %copy-done = f32[3,32,32,128]{3,2,1,0:T(8,128)S(1)} copy-done((f32[3,32,32,128]{3,2,1,0:T(8,128)S(1)}, f32[3,32,32,128]{3,2,1,0:T(8,128)}, u32[]{:S(2)}) %copy-start) | copy-done | bytes 1572888
  33.0 0.1 copy-done.1
  33.1 57.7 %shard_map.78 = (f32[88,128]{1,0:T(8,128)S(1)}, f32[3,32,32,128]{3,2,1,0:T(8,128)S(1)}) custom-call(f32[3,32,32,128]{3,2,1,0:T(8,128)S(1)} %copy-done, f32[32,32,128]{2,1,0:T(8,128)S(1)} %copy-done.1, f32[8,1024]{1,0:T(8,128)S(1)} %broadcast_in_dim.2.row_ref, f32[1024,1]{1,0:T(8,128)S(1)} %fusion.4.col_ref, s32[8,1024]{1,0:T(8,128)S(1)} %pad.12.place_ref, ...), custom_call_target="tpu_custom_call" | custom-call | tf_op jit(solution)/shard_map/pallas_call | solution.py:342
  90.8 0.8 fusion.9
  91.6 1.1 %copy.44 = f32[3,32,32,128]{3,2,1,0:T(8,128)} copy(f32[3,32,32,128]{3,2,1,0:T(8,128)S(1)} %get-tuple-element.11) | data formatting | bytes 3145728
  (9 shorter events, 0.1 us)
Async XLA Ops:
  31.6 1.4 %copy-start = (f32[3,32,32,128]{3,2,1,0:T(8,128)S(1)}, f32[3,32,32,128]{3,2,1,0:T(8,128)}, u32[]{:S(2)}) copy-start(f32[3,32,32,128]{3,2,1,0:T(8,128)} %force_ref.1) | copy-start | bytes 4718596
  31.6 1.5 %copy-start.1 = (f32[32,32,128]{2,1,0:T(8,128)S(1)}, f32[32,32,128]{2,1,0:T(8,128)}, u32[]{:S(2)}) copy-start(f32[32,32,128]{2,1,0:T(8,128)} %shift_ref.1) | copy-start | bytes 1572868
